TPU v7x, 128 devices: a whole 4x4x4 slice. The times are simulated.
128 devices in a mesh: chan: 16 (over x, y_hi, core), band: 8 (over y_lo, z).
Axes of the slice: x: 4, y: 4 (y_hi: 2, y_lo: 2; y = y_hi * 2 + y_lo), z: 4, core: 2. Of those that a mesh axis runs over, the one named last changes fastest.
Arguments:
- strain: float32 [2048, 34816], P(('chan', 'band')), may hold values from -100 to 100
- source_block: int32 [1], replicated, may hold values from 0 to 15
- source_offset: int32 [1], replicated, may hold values from 0 to 127
- window_valid: int32 [16], replicated, may hold values 0 or 1
Outputs:
- correlation: bfloat16 [128, 256, 2048], P('band', None, 'chan')
All inputs are finite; a program needn't handle non-finite values.
Results may differ from a plain program's by a relative error of at most 0.008.
Values may be sent and summed in bfloat16 or wider, within the bound.
A program may use at most 192 MiB of HBM per device.

v0:
```python
import math

import jax
import jax.numpy as jnp
from jax import lax
from jax.sharding import PartitionSpec as P

L = 4096
HOP = 2048
NF = 2048
W = 16
SRC_BLOCK = 128
LAGS = 256


def angle_table(points, bins):
    phase = points[:, None] * bins[None, :] % L
    angle = phase.astype(jnp.float32) * (2.0 * math.pi / L)
    return (jnp.cos(angle), -jnp.sin(angle))


def banded_table(points, first_bin, band_count, band_bins):
    bins = first_bin + jnp.arange(band_count * band_bins, dtype=jnp.int32)
    cosine, sine = angle_table(points, bins)
    shaped = (points.shape[0], band_count, 1, band_bins)
    stacked = jnp.concatenate([cosine.reshape(shaped), sine.reshape(shaped)], axis=2)
    return stacked.reshape(points.shape[0], 2 * band_count * band_bins).astype(jnp.bfloat16)


def taper(strain):
    channels = strain.shape[0]
    halves = strain.reshape(channels, W + 1, HOP)
    segments = jnp.concatenate([halves[:, :-1], halves[:, 1:]], axis=2)
    centred = segments - jnp.mean(segments, axis=2, keepdims=True)
    points = jnp.arange(L, dtype=jnp.float32)
    hann = 0.5 - 0.5 * jnp.cos(points * (2.0 * math.pi / L))
    return (centred * hann).astype(jnp.bfloat16)


def whiten(spectra):
    band_bins = spectra.shape[-1]
    power = jnp.sum(spectra * spectra, axis=(-2, -1), keepdims=True) / band_bins
    return (spectra / jnp.sqrt(power + 1e-06)).astype(jnp.bfloat16)


def product(form, left, right):
    return jnp.einsum(form, left, right, preferred_element_type=jnp.float32)


def cross_lags(block_src, spectra, lag_table, factor):
    real_src = block_src[:, :, :, 0]
    imag_src = block_src[:, :, :, 1]
    real_rec = spectra[:, :, :, 0]
    imag_rec = spectra[:, :, :, 1]
    form = "swbf,cwbf->bfsc"
    cross_real = product(form, real_src, real_rec) + product(form, imag_src, imag_rec)
    cross_imag = product(form, real_src, imag_rec) - product(form, imag_src, real_rec)
    cross = jnp.stack([cross_real, cross_imag], axis=1)
    cross = (cross.reshape(-1, block_src.shape[0], spectra.shape[0]) * factor).astype(jnp.bfloat16)
    return product("tq,qsc->stc", lag_table, cross)


def body(strain, source_block, source_offset, window_valid):
    band_count = lax.axis_size("band")
    chan_count = lax.axis_size("chan")
    own_rows = strain.shape[0]
    chan_rows = own_rows * band_count
    all_rows = chan_rows * chan_count
    band_bins = NF // band_count
    tapered = taper(strain).reshape(own_rows * W, L)
    points = jnp.arange(L, dtype=jnp.int32)

    def band_spectra(band_index):
        basis = banded_table(points, band_index * band_bins, 1, band_bins)
        spectra = jnp.dot(tapered, basis, preferred_element_type=jnp.float32)
        return whiten(spectra.reshape(own_rows, W, 1, 2, band_bins))

    white_bands = lax.map(band_spectra, jnp.arange(band_count, dtype=jnp.int32))
    mine = lax.all_to_all(white_bands, "band", split_axis=0, concat_axis=1, tiled=True)[0]
    offsets = jnp.arange(SRC_BLOCK, dtype=jnp.int32)
    chosen = (
        (source_block[:, None] * SRC_BLOCK + source_offset[:, None] + offsets[None, :]) % all_rows
    ).reshape(-1)
    local_rows = chosen - lax.axis_index("chan") * chan_rows
    columns = jnp.arange(chan_rows, dtype=jnp.int32)
    select = (local_rows[:, None] == columns[None, :]).astype(jnp.bfloat16)
    picked = product("sc,cwbpf->swbpf", select, mine)
    sources = lax.psum(picked.astype(jnp.bfloat16), "chan")
    valid = window_valid.astype(jnp.bfloat16)
    masked = sources * valid[None, :, None, None, None]
    factor = jnp.float32(1.0 / (W * math.sqrt(NF)))
    lags = jnp.arange(LAGS, dtype=jnp.int32) - LAGS // 2
    rows = masked.shape[0] // band_count
    lag_table = banded_table(lags, lax.axis_index("band") * band_bins, 1, band_bins)
    blocks = masked.reshape(lax.axis_size("band") * rows // rows, rows, W, 1, 2, band_bins)

    def one_block(block):
        return cross_lags(block, mine, lag_table, factor)

    total = lax.psum_scatter(
        lax.map(one_block, blocks).reshape(lax.axis_size("band") * rows, LAGS, chan_rows),
        "band",
        scatter_dimension=0,
        tiled=True,
    )
    return total.astype(jnp.bfloat16)


def solution(mesh):
    in_specs = (P(("chan", "band"), None), P(), P(), P())
    out_specs = P("band", None, "chan")
    return jax.shard_map(body, mesh=mesh, in_specs=in_specs, out_specs=out_specs, check_vma=False)
```

profile of v0, /device:TPU:1, one launch (start us, length us, event | category | flops | bytes accessed | tf_op | source)
XLA Modules:
  0.0 669.6 jit_solution(14924427825812940334)
XLA Ops:
  10.9 2.8 fusion.26
  13.7 181.4 %while.24 = (s32[]{:T(128)}, bf16[8,16,16,1,2,256]{5,2,4,3,1,0:T(8,128)(2,1)}, s32[8]{0:T(128)S(1)}, bf16[256,4096]{1,0:T(8,128)(2,1)S(1)}, s32[]{:T(128)}, /*index=5*/s32[1]{0:T(128)}) while((s32[]{:T(128)}, bf16[8,16,16,1,2,256]{5,2,4,3,1,0:T(8,128)(2,1)}, s32[8]{0:T(128)S(1)}, bf16[256,4096]{1,0:T(8,128)(2,1)S(1)}, s32[]{:T(128)}, ...), condition=%wide.region_4.5_spmd.clone, body=%wide.region_2.4_spmd.clone.sunk | while | flops 1094189568 | bytes 22815328 | solution.py:78
  14.9 18.1 %cosine_convert_fusion.3 = (bf16[4096,1,1,256]{0,3,2,1:T(8,128)(2,1)S(1)}, bf16[4096,1,1,256]{0,3,2,1:T(8,128)(2,1)S(1)}) fusion(s32[256]{0:T(256)S(1)} %iota_add_fusion.4), kind=kLoop, calls=%fused_computation.34.clone.1 | loop fusion | flops 17825792 | bytes 4195328 | tf_op jit(solution)/shard_map/convert
  37.5 18.1 %cosine_convert_fusion.3 = (bf16[4096,1,1,256]{0,3,2,1:T(8,128)(2,1)S(1)}, bf16[4096,1,1,256]{0,3,2,1:T(8,128)(2,1)S(1)}) fusion(s32[256]{0:T(256)S(1)} %iota_add_fusion.4), kind=kLoop, calls=%fused_computation.34.clone.1 | loop fusion | flops 17825792 | bytes 4195328 | tf_op jit(solution)/shard_map/convert
  60.2 18.1 %cosine_convert_fusion.3 = (bf16[4096,1,1,256]{0,3,2,1:T(8,128)(2,1)S(1)}, bf16[4096,1,1,256]{0,3,2,1:T(8,128)(2,1)S(1)}) fusion(s32[256]{0:T(256)S(1)} %iota_add_fusion.4), kind=kLoop, calls=%fused_computation.34.clone.1 | loop fusion | flops 17825792 | bytes 4195328 | tf_op jit(solution)/shard_map/convert
  82.9 18.1 %cosine_convert_fusion.3 = (bf16[4096,1,1,256]{0,3,2,1:T(8,128)(2,1)S(1)}, bf16[4096,1,1,256]{0,3,2,1:T(8,128)(2,1)S(1)}) fusion(s32[256]{0:T(256)S(1)} %iota_add_fusion.4), kind=kLoop, calls=%fused_computation.34.clone.1 | loop fusion | flops 17825792 | bytes 4195328 | tf_op jit(solution)/shard_map/convert
  105.6 18.1 %cosine_convert_fusion.3 = (bf16[4096,1,1,256]{0,3,2,1:T(8,128)(2,1)S(1)}, bf16[4096,1,1,256]{0,3,2,1:T(8,128)(2,1)S(1)}) fusion(s32[256]{0:T(256)S(1)} %iota_add_fusion.4), kind=kLoop, calls=%fused_computation.34.clone.1 | loop fusion | flops 17825792 | bytes 4195328 | tf_op jit(solution)/shard_map/convert
  128.2 18.1 %cosine_convert_fusion.3 = (bf16[4096,1,1,256]{0,3,2,1:T(8,128)(2,1)S(1)}, bf16[4096,1,1,256]{0,3,2,1:T(8,128)(2,1)S(1)}) fusion(s32[256]{0:T(256)S(1)} %iota_add_fusion.4), kind=kLoop, calls=%fused_computation.34.clone.1 | loop fusion | flops 17825792 | bytes 4195328 | tf_op jit(solution)/shard_map/convert
  150.9 18.1 %cosine_convert_fusion.3 = (bf16[4096,1,1,256]{0,3,2,1:T(8,128)(2,1)S(1)}, bf16[4096,1,1,256]{0,3,2,1:T(8,128)(2,1)S(1)}) fusion(s32[256]{0:T(256)S(1)} %iota_add_fusion.4), kind=kLoop, calls=%fused_computation.34.clone.1 | loop fusion | flops 17825792 | bytes 4195328 | tf_op jit(solution)/shard_map/convert
  173.6 18.1 %cosine_convert_fusion.3 = (bf16[4096,1,1,256]{0,3,2,1:T(8,128)(2,1)S(1)}, bf16[4096,1,1,256]{0,3,2,1:T(8,128)(2,1)S(1)}) fusion(s32[256]{0:T(256)S(1)} %iota_add_fusion.4), kind=kLoop, calls=%fused_computation.34.clone.1 | loop fusion | flops 17825792 | bytes 4195328 | tf_op jit(solution)/shard_map/convert
  195.1 6.9 %all-to-all-start = ((bf16[8,16,16,1,2,256]{5,2,4,3,1,0:T(8,128)(2,1)}), bf16[8,16,16,1,2,256]{5,2,4,3,1,0:T(8,128)(2,1)S(1)}, u32[]{:S(2)}, u32[]{:S(2)}) async-start(bf16[8,16,16,1,2,256]{5,2,4,3,1,0:T(8,128)(2,1)} %get-tuple-element.98), calls=%async_computation | async-start | bytes 4194304 | tf_op jit(solution)/shard_map/all_to_all | solution.py:79
  203.4 24.8 %all-to-all-done = bf16[8,16,16,1,2,256]{5,2,4,3,1,0:T(8,128)(2,1)S(1)} async-done(((bf16[8,16,16,1,2,256]{5,2,4,3,1,0:T(8,128)(2,1)}), bf16[8,16,16,1,2,256]{5,2,4,3,1,0:T(8,128)(2,1)S(1)}, u32[]{:S(2)}, u32[]{:S(2)}) %all-to-all-start) | async-done | bytes 2097184 | tf_op jit(solution)/shard_map/all_to_all | solution.py:79
  233.6 3.9 copy.54
  237.5 138.2 %all-reduce.2.cloned.1.call-done = bf16[128,16,1,2,256]{4,0,3,1,2:T(8,128)(2,1)} async-done(((bf16[128,16,1,2,256]{4,0,3,1,2:T(8,128)(2,1)}), bf16[128,16,1,2,256]{4,0,3,1,2:T(8,128)(2,1)}) %all-reduce.2.cloned.1.call-update) | async-done | bytes 2097168 | tf_op jit(solution)/shard_map/psum | solution.py:88
  375.7 3.1 broadcast_multiply_fusion
  378.8 108.1 %while.23 = (s32[]{:T(128)}, f32[8,16,256,128]{3,2,1,0:T(8,128)}, bf16[8,16,16,1,2,256]{5,1,0,4,2,3:T(8,128)(2,1)}, bf16[128,16,1,2,256]{0,1,4,3,2:T(8,128)(2,1)}, bf16[256,512]{1,0:T(8,128)(2,1)S(1)}, /*index=5*/s32[]{:T(128)}) while((s32[]{:T(128)}, f32[8,16,256,128]{3,2,1,0:T(8,128)}, bf16[8,16,16,1,2,256]{5,1,0,4,2,3:T(8,128)(2,1)}, ...), condition=%wide.region_7.8_spmd, body=%wide.region_6.7_spmd.sunk | while | flops 608174080 | bytes 49545828 | solution.py:101
  386.5 2.5 fusion.59
  400.0 2.5 fusion.59
  413.5 2.5 fusion.59
  427.0 2.5 fusion.59
  440.5 2.5 fusion.59
  454.1 2.5 fusion.59
  486.9 173.1 %reduce-scatter.2.cloned.1.call-done = f32[16,256,128]{2,1,0:T(8,128)} async-done(((f32[128,256,128]{2,1,0:T(8,128)}), f32[16,256,128]{2,1,0:T(8,128)}) %reduce-scatter.2.cloned.1.call-update) | async-done | bytes 2097168 | tf_op jit(solution)/shard_map/reduce_scatter | solution.py:100
  660.0 2.8 convert_element_type.89
  (193 shorter events, 134.2 us)
Async XLA Ops:
  195.1 33.0 %all-to-all-start = ((bf16[8,16,16,1,2,256]{5,2,4,3,1,0:T(8,128)(2,1)}), bf16[8,16,16,1,2,256]{5,2,4,3,1,0:T(8,128)(2,1)S(1)}, u32[]{:S(2)}, u32[]{:S(2)}) async-start(bf16[8,16,16,1,2,256]{5,2,4,3,1,0:T(8,128)(2,1)} %get-tuple-element.98), calls=%async_computation | async-start | bytes 4194304 | tf_op jit(solution)/shard_map/all_to_all | solution.py:79
  202.0 173.7 %all-reduce.2.cloned.1.call-start = ((), (), s32[]{:S(2)}) async-start(), calls=%async_computation.2 | async-start | bytes 4194304 | tf_op jit(solution)/shard_map/psum | solution.py:88
  231.4 0.7 copy-start.1
  231.4 428.6 %reduce-scatter.2.cloned.1.call-start = ((), (), s32[]{:S(2)}) async-start(), calls=%async_computation.3 | async-start | bytes 18874368 | tf_op jit(solution)/shard_map/reduce_scatter | solution.py:100
  381.9 2.1 copy-start
  395.4 2.1 copy-start
  408.9 2.1 copy-start
  422.4 2.1 copy-start
  435.9 2.1 copy-start
  449.5 2.1 copy-start
  463.0 2.1 copy-start
  476.5 2.1 copy-start
Sparse Core Ops, SparseCore 0:
  231.5 144.1 all-reduce.1
  487.1 172.9 reduce-scatter.1
where the time goes:
time: 670 us
  waiting for transfers between devices  336 us (50%)
  other arithmetic  167 us (25%)
  local copies, waits for them, and re-layouts  74.3 us (11%)
  matrix products  65 us (10%)
  between operations  14.8 us (2%)
  starting transfers between devices  7.14 us (1%)
    reduce_scatter x1, waiting for transfers between devices, body(): lax.psum_scatter(lax.map(one_block, blocks).reshape(lax.axis_size('band')...  173 us
    another operation x9, other arithmetic  146 us
    psum x1, waiting for transfers between devices, body(): sources = lax.psum(picked.astype(jnp.bfloat16), 'chan')  138 us
    dot_general x41, matrix products, product(): return jnp.einsum(form, left, right, preferred_element_type=jnp.float32)  54.6 us
    dynamic_update_slice x16, local copies, waits for them, and re-layouts, body(): lax.map(one_block, blocks)  27.1 us
    all_to_all x1, waiting for transfers between devices, body(): lax.all_to_all(white_bands, 'band', split_axis=0, concat_axis=1, tiled=True)  24.8 us
    dynamic_slice x16, local copies, waits for them, and re-layouts, body(): lax.map(one_block, blocks)  24.3 us
  transfers between devices with their start and end apart: 3, of which 3 were waited for; matrix products, arithmetic and copies ran while one was open for 1% of the time, Pallas kernels for 0%

commit v1 on v0

v1 whole, which is shorter than its diff:
```python
import functools
import math

import jax
import jax.numpy as jnp
import numpy as np
from jax import lax
from jax.experimental import pallas as pl
from jax.experimental.pallas import tpu as pltpu
from jax.sharding import PartitionSpec as P

L = 4096
HOP = 2048
NF = 2048
W = 16
SRC_BLOCK = 128
LAGS = 256
R1 = 32
R2 = 128
HALF = R2 // 2
BINS = 8
FACTOR = 1.0 / (W * math.sqrt(NF))


def window_table():
    points = np.arange(L, dtype=np.float32)
    angle = (points * np.float32(2.0 * math.pi / L)).astype(np.float32)
    return (np.float32(0.5) - np.float32(0.5) * np.cos(angle)).astype(np.float32).reshape(R1, R2)


def twiddle_tables():
    angle = 2.0 * np.pi * np.outer(np.arange(R1), np.arange(R2)) / L
    return np.cos(angle).astype(np.float32), (-np.sin(angle)).astype(np.float32)


def short_dft():
    angle = 2.0 * np.pi * (np.outer(np.arange(HALF), np.arange(R2)) % R2) / R2
    cosine, sine = np.cos(angle), np.sin(angle)
    top = np.concatenate([cosine, sine], axis=1)
    low = np.concatenate([-sine, cosine], axis=1)
    return np.concatenate([top, low], axis=0).astype(np.float32)


def lag_table():
    f1 = np.arange(R1)[:, None, None]
    m = np.arange(4)[None, :, None]
    i = np.arange(16)[None, None, :]
    bins = f1 + R1 * (16 * m + i)
    lags = np.arange(LAGS) - LAGS // 2
    angle = 2.0 * np.pi * ((lags[:, None, None, None] * bins[None]) % L) / L
    table = np.stack([np.cos(angle), -np.sin(angle)], axis=3)
    return table.reshape(LAGS, 2 * NF).astype(np.float32)


def real_dft(x):
    n = len(x)
    if n == 2:
        return [(x[0] + x[1], None), (x[0] - x[1], None)]
    even, odd = real_dft(x[0::2]), real_dft(x[1::2])
    out = [None] * (n // 2 + 1)
    for k in range(n // 4 + 1):
        er, ei = even[k]
        orr, oi = odd[k]
        if k == 0:
            out[0] = (er + orr, None)
            out[n // 2] = (er - orr, None)
            continue
        if 4 * k == n:
            out[k] = (er, -orr)
            continue
        c, s = math.cos(2 * math.pi * k / n), -math.sin(2 * math.pi * k / n)
        if oi is None:
            tr, ti = orr * c, orr * s
        else:
            tr, ti = orr * c - oi * s, orr * s + oi * c
        zi = ti if ei is None else ei + ti
        yi = -ti if ei is None else ei - ti
        out[k] = (er + tr, zi)
        out[n // 2 - k] = (er - tr, -yi)
    return out


def spectra_kernel(strain, hann, tw_cos, tw_sin, dft, mask, white, masked, rows, folded, spectra):
    channels = strain.shape[0]
    pieces = HOP // R2
    for h in range(W + 1):
        for k in range(pieces):
            piece = strain[:, h * HOP + k * R2:h * HOP + (k + 1) * R2]
            if h < W:
                rows[k, pl.ds(h, channels, stride=W), :] = piece
            if h > 0:
                rows[pieces + k, pl.ds(h - 1, channels, stride=W), :] = piece

    def fold(step, _):
        at = pl.ds(pl.multiple_of(step * 16, 16), 16)
        x = [rows[k, at, :] for k in range(R1)]
        total = x[0]
        for k in range(1, R1):
            total = total + x[k]
        mean = jnp.sum(total, axis=1, keepdims=True) * (1.0 / L)
        x = [((x[k] - mean) * hann[k:k + 1, :]).astype(jnp.bfloat16).astype(jnp.float32) for k in range(R1)]
        bins = real_dft(x)
        for f in range(R1):
            re, im = bins[f] if f <= R1 // 2 else bins[R1 - f]
            if im is None:
                gr, gi = re * tw_cos[f:f + 1, :], re * tw_sin[f:f + 1, :]
            else:
                im = im if f <= R1 // 2 else -im
                c, s = tw_cos[f:f + 1, :], tw_sin[f:f + 1, :]
                gr, gi = re * c - im * s, re * s + im * c
            folded[f, at, :] = jnp.concatenate([gr, gi], axis=1).astype(jnp.bfloat16)
        return 0

    lax.fori_loop(0, channels * W // 16, fold, 0)
    table = dft[...]

    def transform(f, power):
        y = lax.dot_general(table, folded[f], (((1,), (1,)), ((), ())), preferred_element_type=jnp.float32)
        spectra[f] = y
        return power + y * y

    power = lax.fori_loop(0, R1, transform, jnp.zeros((R2, channels * W), jnp.float32))
    scales = []
    for b in range(HALF // BINS):
        both = power[b * BINS:(b + 1) * BINS] + power[HALF + b * BINS:HALF + (b + 1) * BINS]
        total = jnp.sum(both, axis=0, keepdims=True) * (1.0 / 256.0)
        scales.append(jnp.broadcast_to(lax.rsqrt(total + 1e-06), both.shape))
    scale = jnp.concatenate(scales + scales, axis=0)
    keep = mask[...]

    def finish(f, _):
        value = (spectra[f] * scale).astype(jnp.bfloat16)
        white[f] = value
        masked[f] = (value.astype(jnp.float32) * keep).astype(jnp.bfloat16)
        return 0

    lax.fori_loop(0, R1, finish, 0)


def whiten(strain, mask):
    channels = strain.shape[0]
    lanes = channels * W
    tw_cos, tw_sin = twiddle_tables()
    shape = jax.ShapeDtypeStruct((R1, R2, lanes), jnp.bfloat16)
    return pl.pallas_call(
        spectra_kernel,
        out_shape=(shape, shape),
        scratch_shapes=[
            pltpu.VMEM((R1, lanes, R2), jnp.float32),
            pltpu.VMEM((R1, lanes, 2 * R2), jnp.bfloat16),
            pltpu.VMEM((R1, R2, lanes), jnp.float32),
        ],
        compiler_params=pltpu.CompilerParams(vmem_limit_bytes=48 * 2**20),
        cost_estimate=pl.CostEstimate(flops=2 * 32 * 128 * 256 * 256, bytes_accessed=8 * 2**20, transcendentals=0),
    )(strain, jnp.asarray(window_table()), jnp.asarray(tw_cos), jnp.asarray(tw_sin),
      jnp.asarray(short_dft(), dtype=jnp.bfloat16), mask)


CHUNK = 4


def lag_kernel(white, sources, table, out, total, cross):
    step = pl.program_id(0)
    row = lax.broadcasted_iota(jnp.int32, (BINS, R2), 0)
    lane = lax.broadcasted_iota(jnp.int32, (BINS, R2), 1)
    own = lane // W == row
    channels = white.shape[2] // W

    def slanted(x):
        return [pltpu.roll(x[:, k * R2:(k + 1) * R2], 0, 1, stride=W, stride_axis=0) for k in range(channels // 8)]

    def spread(x, c):
        part = x[c // 8]
        rolled = pltpu.roll(part, R2 - W * (c % 8), 1) if c % 8 else part
        return jnp.where(own, rolled, 0.0)

    def pair(index, _):
        f, m = index // 4, index % 4
        re = white[f, pl.ds(pl.multiple_of(m * 16, 16), 16), :].astype(jnp.float32)
        im = white[f, pl.ds(pl.multiple_of(HALF + m * 16, 16), 16), :].astype(jnp.float32)
        results = []
        for g in range(2):
            xr, xi = slanted(re[g * 8:(g + 1) * 8]), slanted(im[g * 8:(g + 1) * 8])
            left = jnp.concatenate(
                [jnp.concatenate([spread(xr, c), spread(xi, c)], axis=1) for c in range(channels)], axis=0
            ).astype(jnp.bfloat16)
            s = sources[index * 2 + g]
            sr, si = s[:R2], s[R2:]
            right = jnp.concatenate([s, jnp.concatenate([-si, sr], axis=0)], axis=1)
            results.append(jnp.dot(left, right, preferred_element_type=jnp.float32) * FACTOR)
        base = pl.multiple_of(index * 32, 32)
        for c in range(channels):
            both = jnp.concatenate([r[c * 8:(c + 1) * 8] for r in results], axis=0).astype(jnp.bfloat16)
            cross[pl.ds(base, 16), c * SRC_BLOCK:(c + 1) * SRC_BLOCK] = both[:, :SRC_BLOCK]
            cross[pl.ds(base + 16, 16), c * SRC_BLOCK:(c + 1) * SRC_BLOCK] = both[:, SRC_BLOCK:]
        return 0

    lax.fori_loop(0, CHUNK * 4, pair, 0)
    part = table[...]
    width = 256

    @pl.when(step == 0)
    def _():
        total[...] = jnp.zeros_like(total)

    def columns(n, _):
        at = pl.ds(pl.multiple_of(n * width, width), width)
        total[:, at] += jnp.dot(part, cross[:, at], preferred_element_type=jnp.float32)
        return 0

    lax.fori_loop(0, total.shape[1] // width, columns, 0)

    @pl.when(step == pl.num_programs(0) - 1)
    def _():
        out[...] = total[...].astype(out.dtype)


def correlate(white, sources):
    channels = white.shape[2] // W
    columns = channels * SRC_BLOCK
    depth = CHUNK * R2
    return pl.pallas_call(
        lag_kernel,
        grid=(R1 // CHUNK,),
        in_specs=[
            pl.BlockSpec((CHUNK, R2, channels * W), lambda i: (i, 0, 0)),
            pl.BlockSpec((CHUNK * 8, 2 * R2, SRC_BLOCK), lambda i: (i, 0, 0)),
            pl.BlockSpec((LAGS, depth), lambda i: (0, i)),
        ],
        out_specs=pl.BlockSpec((LAGS, columns), lambda i: (0, 0)),
        out_shape=jax.ShapeDtypeStruct((LAGS, columns), jnp.bfloat16),
        scratch_shapes=[
            pltpu.VMEM((LAGS, columns), jnp.float32),
            pltpu.VMEM((depth, columns), jnp.bfloat16),
        ],
        compiler_params=pltpu.CompilerParams(vmem_limit_bytes=48 * 2**20),
        cost_estimate=pl.CostEstimate(flops=2 * 256 * 4096 * 2048, bytes_accessed=20 * 2**20, transcendentals=0),
    )(white, sources, jnp.asarray(lag_table(), dtype=jnp.bfloat16))


def body(strain, source_block, source_offset, window_valid):
    own_rows = strain.shape[0]
    bands = lax.axis_size("band")
    chans = lax.axis_size("chan")
    block, offset = source_block[0], source_offset[0]
    row = lax.axis_index("band") * own_rows + jnp.arange(own_rows, dtype=jnp.int32)
    chan = lax.axis_index("chan")
    held = ((chan == block) & (row >= offset)) | ((chan == (block + 1) % chans) & (row < offset))
    mask = (held[:, None] & (window_valid != 0)[None, :]).astype(jnp.float32).reshape(1, own_rows * W)
    white, masked = whiten(strain, mask)

    per = R1 // chans
    parts = lax.all_to_all(masked, "chan", split_axis=0, concat_axis=0, tiled=True)
    piece = jnp.sum(parts.reshape(chans, per, R2, own_rows * W).astype(jnp.float32), axis=0).astype(jnp.bfloat16)
    piece = piece.reshape(per, 2, 4, 16, own_rows * W).transpose(0, 2, 1, 3, 4).reshape(bands, 2, 16, own_rows * W)
    piece = lax.all_to_all(piece, "band", split_axis=0, concat_axis=0, tiled=True)
    piece = piece.reshape(bands, 2, 2, BINS, own_rows, W).transpose(2, 1, 3, 5, 0, 4)
    piece = jnp.roll(piece.reshape(2, 2 * BINS * W, SRC_BLOCK), -offset, axis=2)
    sources = lax.all_gather(piece, ("chan", "band"), axis=0, tiled=True)

    total = correlate(white, sources)
    total = total.reshape(LAGS, own_rows, bands, SRC_BLOCK // bands).transpose(2, 3, 0, 1)
    total = lax.all_to_all(total, "band", split_axis=0, concat_axis=0, tiled=False)
    return total.transpose(1, 2, 0, 3).reshape(SRC_BLOCK // bands, LAGS, bands * own_rows)


def solution(mesh):
    in_specs = (P(("chan", "band"), None), P(), P(), P())
    out_specs = P("band", None, "chan")
    return jax.shard_map(body, mesh=mesh, in_specs=in_specs, out_specs=out_specs, check_vma=False)
```

time: 670 us -> 493 us (0.74)
  other arithmetic: 167 us -> 1.84 us
  Pallas kernels: 0 us -> 71.7 us
  matrix products: 65 us -> 0 us
  local copies, waits for them, and re-layouts: 74.3 us -> 11.8 us
  blocking collectives: 0 us -> 56.1 us
    all_gather x0 -> x1, waiting for transfers between devices: none -> 325 us  [body(): sources = lax.all_gather(piece, ('chan', 'band'), axis=0, tiled=True)]
    reduce_scatter x1 -> x0, waiting for transfers between devices: 173 us -> none  [body(): lax.psum_scatter(lax.map(one_block, blocks).reshape(lax.axis_size('band')...]
    another operation x9 -> x0, other arithmetic: 146 us -> none
    psum x1 -> x0, waiting for transfers between devices: 138 us -> none  [body(): sources = lax.psum(picked.astype(jnp.bfloat16), 'chan')]
    pallas_call x0 -> x2, Pallas kernels: none -> 71.7 us  [the longest x1 56.4 us: correlate(): pl.pallas_call(lag_kernel, grid=(R1 // CHUNK,), in_specs=[pl.BlockSpec((C...]
    dot_general x49 -> x0, matrix products: 65 us -> none  [the longest x41 54.6 us: product(): return jnp.einsum(form, left, right, preferred_element_type=jnp.float32)]
    all_to_all x0 -> x2, blocking collectives: none -> 56.1 us  [the longest x1 36.2 us: body(): lax.all_to_all(masked, 'chan', split_axis=0, concat_axis=0, tiled=True)]
    dynamic_update_slice x24 -> x0, local copies, waits for them, and re-layouts: 33 us -> none  [the longest x16 27.1 us: body(): lax.map(one_block, blocks)]
  transfers between devices with their start and end apart: 3 -> 2, of which waited for: 3 -> 2; matrix products, arithmetic and copies ran while one was open for 1% -> 0% of each run, Pallas kernels for 0% -> 0%
where the time goes in v1:
time: 493 us; the launch traced here: 492 us
  waiting for transfers between devices  330 us (67%)
  Pallas kernels  71.7 us (15%)
  blocking collectives  56.1 us (11%)
  between operations  14.8 us (3%)
  local copies, waits for them, and re-layouts  11.8 us (2%)
  starting transfers between devices  5.18 us (1%)
    all_gather x1, waiting for transfers between devices, body(): sources = lax.all_gather(piece, ('chan', 'band'), axis=0, tiled=True)  325 us
    pallas_call x1, Pallas kernels, correlate(): pl.pallas_call(lag_kernel, grid=(R1 // CHUNK,), in_specs=[pl.BlockSpec((C...  56.4 us
    all_to_all x1, blocking collectives, body(): lax.all_to_all(masked, 'chan', split_axis=0, concat_axis=0, tiled=True)  36.2 us
    all_to_all x1, blocking collectives, body(): lax.all_to_all(total, 'band', split_axis=0, concat_axis=0, tiled=False)  19.9 us
    pallas_call x1, Pallas kernels, whiten(): pl.pallas_call(spectra_kernel, out_shape=(shape, shape), scratch_shapes=[...  15.3 us
  transfers between devices with their start and end apart: 2, of which 2 were waited for; matrix products, arithmetic and copies ran while one was open for 0% of the time, Pallas kernels for 0%

profile of v1, /device:TPU:1, one launch (start us, length us, event | category | flops | bytes accessed | tf_op | source)
XLA Modules:
  0.0 491.9 jit_solution(10136785558103708282)
XLA Ops:
  7.9 0.7 and_or_fusion
  8.5 0.1 and_convert_fusion
  8.6 0.1 reshape.66.mask
  8.7 0.8 copy-done.3
  9.5 0.7 copy-done.4
  10.2 0.7 copy-done.5
  11.0 0.7 copy-done.6
  11.7 15.3 %shard_map.91 = (bf16[32,128,256]{2,1,0:T(8,128)(2,1)S(1)}, bf16[32,128,256]{2,1,0:T(8,128)(2,1)S(1)}) custom-call(f32[16,34816]{1,0:T(8,128)} %strain.1, f32[32,128]{1,0:T(8,128)S(1)} %copy-done.6, f32[32,128]{1,0:T(8,128)S(1)} %copy-done.5, f32[32,128]{1,0:T(8,128)S(1)} %copy-done.4, bf16[128,256]{1,0:T(8,128)(2,1)S(1)} %copy-done.3, ...), custom_call_target="tpu_custom_call" | custom-call | flops 536870912 | bytes 8388608 | tf_op jit(solution)/shard_map/pallas_call | solution.py:145
  27.0 36.2 %all_to_all.15 = bf16[32,128,256]{2,1,0:T(8,128)(2,1)S(1)} all-to-all(bf16[32,128,256]{2,1,0:T(8,128)(2,1)S(1)} %get-tuple-element.8), channel_id=1, replica_groups=mesh['chan'=16,'band'=8] {'chan'}, dimensions={0} | all-to-all | bytes 4194304 | tf_op jit(solution)/shard_map/all_to_all | solution.py:253
  63.2 0.3 reduce_sum.12
  63.5 0.7 copy.25
  64.1 5.1 %all-to-all-start.1 = ((bf16[8,2,16,256]{3,2,1,0:T(8,128)(2,1)}), bf16[8,2,16,256]{3,2,1,0:T(8,128)(2,1)S(1)}, u32[]{:S(2)}, u32[]{:S(2)}) async-start(bf16[8,2,16,256]{3,2,1,0:T(8,128)(2,1)} %bitcast.5), calls=%async_computation.1 | async-start | bytes 262144 | tf_op jit(solution)/shard_map/all_to_all | solution.py:256
  69.4 5.4 %all-to-all-done.1 = bf16[8,2,16,256]{3,2,1,0:T(8,128)(2,1)S(1)} async-done(((bf16[8,2,16,256]{3,2,1,0:T(8,128)(2,1)}), bf16[8,2,16,256]{3,2,1,0:T(8,128)(2,1)S(1)}, u32[]{:S(2)}, u32[]{:S(2)}) %all-to-all-start.1) | async-done | bytes 131104 | tf_op jit(solution)/shard_map/all_to_all | solution.py:256
  74.7 0.7 reshape.62
  75.4 1.5 copy.26
  76.9 2.0 reshape.63
  78.9 0.8 fusion
  79.8 325.1 %all-gather.2.cloned.1.call-done.sources = bf16[256,256,128]{2,1,0:T(8,128)(2,1)} async-done(((bf16[2,256,128]{2,1,0:T(8,128)(2,1)}), bf16[256,256,128]{2,1,0:T(8,128)(2,1)}) %all-gather.2.cloned.1.call-update) | async-done | bytes 16777232 | tf_op jit(solution)/shard_map/all_gather | solution.py:259
  404.9 1.6 copy-done.2
  406.4 56.4 %shard_map.92 = bf16[256,2048]{1,0:T(8,128)(2,1)S(1)} custom-call(bf16[32,128,256]{2,1,0:T(8,128)(2,1)S(1)} %copy-done.2, bf16[256,256,128]{2,1,0:T(8,128)(2,1)} %all-gather.2.cloned.1.call-done.sources, bf16[256,4096]{1,0:T(8,128)(2,1)S(1)} %copy-done), custom_call_target="tpu_custom_call" | custom-call | flops 4294967296 | bytes 20971520 | tf_op jit(solution)/shard_map/pallas_call | solution.py:222
  462.9 0.5 copy.27
  463.4 0.1 copy.28
  463.5 19.9 %all_to_all.16 = bf16[8,16,256,16]{2,1,3,0:T(8,128)(2,1)S(1)} all-to-all(bf16[8,16,256,16]{2,1,3,0:T(8,128)(2,1)S(1)} %copy.28), channel_id=1, replica_groups=mesh['chan'=16,'band'=8] {'band'}, dimensions={0} | all-to-all | bytes 2097152 | tf_op jit(solution)/shard_map/all_to_all | solution.py:263
  483.4 1.7 copy.30
  (11 shorter events, 0.1 us)
Async XLA Ops:
  8.7 0.8 copy-start.3
  9.5 0.7 copy-start.4
  10.2 0.7 copy-start.5
  11.0 0.7 copy-start.6
  26.9 36.2 %copy-start.1 = (bf16[32,128,256]{2,1,0:T(8,128)(2,1)}, bf16[32,128,256]{2,1,0:T(8,128)(2,1)S(1)}, u32[]{:S(2)}) copy-start(bf16[32,128,256]{2,1,0:T(8,128)(2,1)S(1)} %get-tuple-element.7.white) | copy-start | bytes 6291460
  64.1 10.6 %all-to-all-start.1 = ((bf16[8,2,16,256]{3,2,1,0:T(8,128)(2,1)}), bf16[8,2,16,256]{3,2,1,0:T(8,128)(2,1)S(1)}, u32[]{:S(2)}, u32[]{:S(2)}) async-start(bf16[8,2,16,256]{3,2,1,0:T(8,128)(2,1)} %bitcast.5), calls=%async_computation.1 | async-start | bytes 262144 | tf_op jit(solution)/shard_map/all_to_all | solution.py:256
  69.3 335.6 %all-gather.2.cloned.1.call-start = ((), (), s32[]{:S(2)}) async-start(), calls=%async_computation.3 | async-start | bytes 16908288 | tf_op jit(solution)/shard_map/all_gather | solution.py:259
  75.4 329.4 %copy-start = (bf16[256,4096]{1,0:T(8,128)(2,1)S(1)}, bf16[256,4096]{1,0:T(8,128)(2,1)}, u32[]{:S(2)}) copy-start(bf16[256,4096]{1,0:T(8,128)(2,1)} %constant.63.clone.table) | copy-start | bytes 6291460
  404.9 1.6 copy-start.2
Sparse Core Ops, SparseCore 0:
  79.9 324.9 all-gather.1

commit v2 on v1

--- a/solution.py
+++ b/solution.py
@@ -42,14 +42,12 @@
 
 
 def lag_table():
-    f1 = np.arange(R1)[:, None, None]
-    m = np.arange(4)[None, :, None]
-    i = np.arange(16)[None, None, :]
-    bins = f1 + R1 * (16 * m + i)
-    lags = np.arange(LAGS) - LAGS // 2
-    angle = 2.0 * np.pi * ((lags[:, None, None, None] * bins[None]) % L) / L
-    table = np.stack([np.cos(angle), -np.sin(angle)], axis=3)
-    return table.reshape(LAGS, 2 * NF).astype(np.float32)
+    core, g, x, y_hi, y_lo, z_hi, z_lo, i = np.ix_(*[np.arange(n) for n in (2, 2, 4, 2, 2, 2, 2, 8)])
+    bins = 8 * x + 4 * y_hi + 2 * core + y_lo + R1 * (16 * (2 * z_hi + z_lo) + 8 * g + i)
+    lags = (np.arange(LAGS) - LAGS // 2).reshape((1, LAGS) + (1,) * 7)
+    angle = 2.0 * np.pi * (lags * bins[:, None] % L) / L
+    table = np.stack([np.cos(angle), -np.sin(angle)], axis=7)
+    return table.reshape(2, LAGS, NF).astype(np.float32)
 
 
 def real_dft(x):
@@ -156,86 +154,240 @@
       jnp.asarray(short_dft(), dtype=jnp.bfloat16), mask)
 
 
-CHUNK = 4
-
-
-def lag_kernel(white, sources, table, out, total, cross):
-    step = pl.program_id(0)
-    row = lax.broadcasted_iota(jnp.int32, (BINS, R2), 0)
-    lane = lax.broadcasted_iota(jnp.int32, (BINS, R2), 1)
+SIDE = 4
+SLOTS = SIDE ** 3
+PIECE = 2 * 2 * BINS * W
+PARTS = ((0, 48, 48, (0, 1, 2)), (96, 48, 32, (1, 2, 0)), (176, 32, 48, (2, 0, 1)))
+ROUNDS = 2
+MESH = pl.DeviceIdType.MESH
+
+
+def position():
+    chan, band = lax.axis_index("chan"), lax.axis_index("band")
+    return (chan // 4, chan // 2 % 2 * 2 + band // 4, band % 4), chan % 2
+
+
+def device_at(at, core):
+    x, y, z = at
+    return (x * 4 + y // 2 * 2 + core, y % 2 * 4 + z)
+
+
+def neighbour(axis, step):
+    at, core = position()
+    moved = list(at)
+    moved[axis] = lax.rem(at[axis] + step + SIDE, SIDE)
+    return device_at(moved, core)
+
+
+def slots(ref, at, full, first, count):
+    whole = slice(None)
+    x = whole if 0 in full else at[0]
+    y_hi, y_lo = (whole, whole) if 1 in full else (at[1] // 2, at[1] % 2)
+    z = whole if 2 in full else at[2]
+    return ref.at[x, y_hi, y_lo, z, pl.ds(first, count), :]
+
+
+def lag_kernel(white, piece, tables, out, spectra, held, left, cross, total, table, outgoing, incoming,
+               local_sem, send_sem, recv_sem, side_send, side_recv):
+    at, core = position()
+    sibling = device_at(at, 1 - core)
+    columns = out.shape[1]
+    channels = columns // SRC_BLOCK
+
+    own_piece = pltpu.make_async_copy(piece, spectra.at[at[0], at[1] // 2, at[1] % 2, at[2]], local_sem.at[0])
+    own_white = pltpu.make_async_copy(white.at[:, core], held.at[0], local_sem.at[1])
+    own_table = pltpu.make_async_copy(tables.at[core], table, local_sem.at[2])
+    own_piece.start()
+    own_white.start()
+    own_table.start()
+
+    barrier = pltpu.get_barrier_semaphore()
+    for axis in range(3):
+        for step in (1, -1):
+            pl.semaphore_signal(barrier, inc=1, device_id=neighbour(axis, step), device_id_type=MESH)
+    pl.semaphore_signal(barrier, inc=1, device_id=sibling, device_id_type=MESH)
+    pl.semaphore_wait(barrier, 7)
+
+    other_white = pltpu.make_async_remote_copy(
+        src_ref=white.at[:, 1 - core], dst_ref=held.at[1], send_sem=side_send.at[0], recv_sem=side_recv.at[0],
+        device_id=sibling, device_id_type=MESH)
+    other_white.start()
+    own_piece.wait()
+
+    copies = {}
+
+    def start(turn, stage, part, kind):
+        first, low, high, order = PARTS[part]
+        first += turn * (PIECE // ROUNDS)
+        axis, full = order[stage], order[:stage]
+        if kind < 2:
+            ref = slots(spectra, at, full, first, low + high)
+        else:
+            moved = list(at)
+            moved[axis] = lax.rem(at[axis] + (SIDE - 1 if kind == 2 else 1), SIDE)
+            ref = slots(spectra, moved, full, first + (0 if kind == 2 else low), low if kind == 2 else high)
+        slot = ((turn * 3 + stage) * 3 + part) * 4 + kind
+        copy = pltpu.make_async_remote_copy(
+            src_ref=ref, dst_ref=ref, send_sem=send_sem.at[slot], recv_sem=recv_sem.at[slot],
+            device_id=neighbour(axis, 1 if kind % 2 == 0 else -1), device_id_type=MESH)
+        copies[turn, stage, part, kind] = copy
+        copy.start()
+
+    def begin(turn, stage):
+        for part in range(3):
+            start(turn, stage, part, 0)
+            start(turn, stage, part, 1)
+
+    def forward(turn, stage):
+        for part in range(3):
+            copies[turn, stage, part, 0].wait_recv()
+            start(turn, stage, part, 2)
+            copies[turn, stage, part, 1].wait_recv()
+            start(turn, stage, part, 3)
+
+    def finish(turn, stage):
+        for part in range(3):
+            copies[turn, stage, part, 2].wait_recv()
+            copies[turn, stage, part, 3].wait_recv()
+
+    row = lax.broadcasted_iota(jnp.int32, (2 * BINS, R2), 0) % BINS
+    lane = lax.broadcasted_iota(jnp.int32, (2 * BINS, R2), 1)
     own = lane // W == row
-    channels = white.shape[2] // W
-
-    def slanted(x):
-        return [pltpu.roll(x[:, k * R2:(k + 1) * R2], 0, 1, stride=W, stride_axis=0) for k in range(channels // 8)]
-
-    def spread(x, c):
-        part = x[c // 8]
-        rolled = pltpu.roll(part, R2 - W * (c % 8), 1) if c % 8 else part
-        return jnp.where(own, rolled, 0.0)
-
-    def pair(index, _):
-        f, m = index // 4, index % 4
-        re = white[f, pl.ds(pl.multiple_of(m * 16, 16), 16), :].astype(jnp.float32)
-        im = white[f, pl.ds(pl.multiple_of(HALF + m * 16, 16), 16), :].astype(jnp.float32)
-        results = []
-        for g in range(2):
-            xr, xi = slanted(re[g * 8:(g + 1) * 8]), slanted(im[g * 8:(g + 1) * 8])
-            left = jnp.concatenate(
-                [jnp.concatenate([spread(xr, c), spread(xi, c)], axis=1) for c in range(channels)], axis=0
-            ).astype(jnp.bfloat16)
-            s = sources[index * 2 + g]
-            sr, si = s[:R2], s[R2:]
-            right = jnp.concatenate([s, jnp.concatenate([-si, sr], axis=0)], axis=1)
-            results.append(jnp.dot(left, right, preferred_element_type=jnp.float32) * FACTOR)
-        base = pl.multiple_of(index * 32, 32)
-        for c in range(channels):
-            both = jnp.concatenate([r[c * 8:(c + 1) * 8] for r in results], axis=0).astype(jnp.bfloat16)
-            cross[pl.ds(base, 16), c * SRC_BLOCK:(c + 1) * SRC_BLOCK] = both[:, :SRC_BLOCK]
-            cross[pl.ds(base + 16, 16), c * SRC_BLOCK:(c + 1) * SRC_BLOCK] = both[:, SRC_BLOCK:]
-        return 0
-
-    lax.fori_loop(0, CHUNK * 4, pair, 0)
-    part = table[...]
-    width = 256
-
-    @pl.when(step == 0)
-    def _():
-        total[...] = jnp.zeros_like(total)
-
-    def columns(n, _):
-        at = pl.ds(pl.multiple_of(n * width, width), width)
-        total[:, at] += jnp.dot(part, cross[:, at], preferred_element_type=jnp.float32)
-        return 0
-
-    lax.fori_loop(0, total.shape[1] // width, columns, 0)
-
-    @pl.when(step == pl.num_programs(0) - 1)
-    def _():
-        out[...] = total[...].astype(out.dtype)
-
-
-def correlate(white, sources):
-    channels = white.shape[2] // W
-    columns = channels * SRC_BLOCK
-    depth = CHUNK * R2
+
+    def spread(core_index):
+        def step(index, _):
+            x, y_hi, y_lo, z = index // 16, index // 8 % 2, index // 4 % 2, index % 4
+            for ri in range(2):
+                rows = pl.ds(pl.multiple_of(ri * HALF + z * 16, 16), 16)
+                for k in range(channels // 8):
+                    value = held[core_index, x * 2 + y_hi, y_lo, rows, k * R2:(k + 1) * R2].astype(jnp.float32)
+                    for g in range(2):
+                        even = pltpu.roll(value[g * BINS:(g + 1) * BINS], 0, 1, stride=W, stride_axis=0)
+                        both = jnp.concatenate([even, pltpu.roll(even, R2 - W, 1)], axis=0)
+                        for t in range(4):
+                            moved = pltpu.roll(both, R2 - 2 * W * t, 1) if t else both
+                            first = ((core_index * channels // 8 + k) * 4 + t) * 2 * BINS
+                            left[g, index, first:first + 2 * BINS, ri * R2:(ri + 1) * R2] = jnp.where(
+                                own, moved, 0.0).astype(jnp.bfloat16)
+            return 0
+
+        return step
+
+    def multiply(turn):
+        def step(index, _):
+            results = []
+            for h in range(2):
+                slot = index * 2 + h
+                s = spectra[slot // 16, slot // 8 % 2, slot // 4 % 2, slot % 4, turn * 256:(turn + 1) * 256, :]
+                right = jnp.concatenate([s, jnp.concatenate([-s[R2:], s[:R2]], axis=0)], axis=1)
+                results.append(jnp.dot(left[turn, slot], right, preferred_element_type=jnp.float32))
+            base = pl.multiple_of(index * 32, 32)
+            for c in range(2 * channels):
+                both = jnp.concatenate([r[c * BINS:(c + 1) * BINS] for r in results], axis=0).astype(jnp.bfloat16)
+                cross[pl.ds(base, 16), c * SRC_BLOCK:(c + 1) * SRC_BLOCK] = both[:, :SRC_BLOCK]
+                cross[pl.ds(base + 16, 16), c * SRC_BLOCK:(c + 1) * SRC_BLOCK] = both[:, SRC_BLOCK:]
+            return 0
+
+        return step
+
+    width = 1024
+
+    def sum_lags(turn, core_index, store):
+        def step(n, _):
+            to = pl.ds(pl.multiple_of(n * width, width), width)
+            both = pl.ds(pl.multiple_of(core_index * columns + n * width, width), width)
+            store(to, both, jnp.dot(table[:, turn * 1024:(turn + 1) * 1024], cross[:, both],
+                                    preferred_element_type=jnp.float32))
+            return 0
+
+        lax.fori_loop(0, columns // width, step, 0)
+
+    def keep(to, both, value):
+        total[:, both] = value
+
+    def hand_over(to, both, value):
+        outgoing[:, to] = ((total[:, both] + value) * FACTOR).astype(jnp.bfloat16)
+
+    def conclude(to, both, value):
+        total[:, both] = total[:, both] + value
+
+    pairs = SLOTS // 2
+    begin(0, 0)
+    own_white.wait()
+    lax.fori_loop(0, 6, spread(0), 0)
+    forward(0, 0)
+    lax.fori_loop(6, 10, spread(0), 0)
+    finish(0, 0)
+    begin(0, 1)
+    begin(1, 0)
+    lax.fori_loop(10, 22, spread(0), 0)
+    forward(0, 1)
+    forward(1, 0)
+    lax.fori_loop(22, 30, spread(0), 0)
+    finish(0, 1)
+    finish(1, 0)
+    begin(0, 2)
+    begin(1, 1)
+    lax.fori_loop(30, SLOTS, spread(0), 0)
+    other_white.wait_recv()
+    lax.fori_loop(0, 16, spread(1), 0)
+    forward(1, 1)
+    forward(0, 2)
+    finish(1, 1)
+    lax.fori_loop(16, SLOTS, spread(1), 0)
+    finish(0, 2)
+    begin(1, 2)
+    own_table.wait()
+    lax.fori_loop(0, pairs, multiply(0), 0, unroll=2)
+    forward(1, 2)
+    sum_lags(0, 0, keep)
+    sum_lags(0, 1, keep)
+    finish(1, 2)
+    lax.fori_loop(0, pairs, multiply(1), 0, unroll=2)
+    sum_lags(1, 1, hand_over)
+    exchange = pltpu.make_async_remote_copy(
+        src_ref=outgoing, dst_ref=incoming, send_sem=side_send.at[1], recv_sem=side_recv.at[1],
+        device_id=sibling, device_id_type=MESH)
+    exchange.start()
+    sum_lags(1, 0, conclude)
+    exchange.wait()
+    out[...] = (total[:, :columns] * FACTOR + incoming[...].astype(jnp.float32)).astype(out.dtype)
+    other_white.wait_send()
+    for copy in copies.values():
+        copy.wait_send()
+
+
+def correlate(white, piece):
+    lanes = white.shape[2]
+    columns = lanes // W * SRC_BLOCK
+    grouped = white.reshape(SIDE * 2, 2, 2, R2, lanes)
+    half = 2 * NF // 2
+    copies = ROUNDS * 3 * 3 * 4
+    anywhere = pl.BlockSpec(memory_space=pl.ANY)
     return pl.pallas_call(
         lag_kernel,
-        grid=(R1 // CHUNK,),
-        in_specs=[
-            pl.BlockSpec((CHUNK, R2, channels * W), lambda i: (i, 0, 0)),
-            pl.BlockSpec((CHUNK * 8, 2 * R2, SRC_BLOCK), lambda i: (i, 0, 0)),
-            pl.BlockSpec((LAGS, depth), lambda i: (0, i)),
-        ],
-        out_specs=pl.BlockSpec((LAGS, columns), lambda i: (0, 0)),
+        in_specs=[anywhere] * 3,
+        out_specs=pl.BlockSpec(memory_space=pltpu.VMEM),
         out_shape=jax.ShapeDtypeStruct((LAGS, columns), jnp.bfloat16),
         scratch_shapes=[
-            pltpu.VMEM((LAGS, columns), jnp.float32),
-            pltpu.VMEM((depth, columns), jnp.bfloat16),
+            pltpu.VMEM((SIDE, 2, 2, SIDE, PIECE, SRC_BLOCK), jnp.bfloat16),
+            pltpu.VMEM((2, SIDE * 2, 2, R2, lanes), jnp.bfloat16),
+            pltpu.VMEM((2, SLOTS, 256, 256), jnp.bfloat16),
+            pltpu.VMEM((half // 2, 2 * columns), jnp.bfloat16),
+            pltpu.VMEM((LAGS, 2 * columns), jnp.float32),
+            pltpu.VMEM((LAGS, half), jnp.bfloat16),
+            pltpu.VMEM((LAGS, columns), jnp.bfloat16),
+            pltpu.VMEM((LAGS, columns), jnp.bfloat16),
+            pltpu.SemaphoreType.DMA((3,)),
+            pltpu.SemaphoreType.DMA((copies,)),
+            pltpu.SemaphoreType.DMA((copies,)),
+            pltpu.SemaphoreType.DMA((2,)),
+            pltpu.SemaphoreType.DMA((2,)),
         ],
-        compiler_params=pltpu.CompilerParams(vmem_limit_bytes=48 * 2**20),
-        cost_estimate=pl.CostEstimate(flops=2 * 256 * 4096 * 2048, bytes_accessed=20 * 2**20, transcendentals=0),
-    )(white, sources, jnp.asarray(lag_table(), dtype=jnp.bfloat16))
+        compiler_params=pltpu.CompilerParams(
+            vmem_limit_bytes=60 * 2**20, collective_id=1, has_side_effects=True),
+        cost_estimate=pl.CostEstimate(flops=4 * 256 * 4096 * 2048, bytes_accessed=20 * 2**20, transcendentals=0),
+    )(grouped, piece, jnp.asarray(lag_table(), dtype=jnp.bfloat16))
 
 
 def body(strain, source_block, source_offset, window_valid):
@@ -256,9 +408,7 @@
     piece = lax.all_to_all(piece, "band", split_axis=0, concat_axis=0, tiled=True)
     piece = piece.reshape(bands, 2, 2, BINS, own_rows, W).transpose(2, 1, 3, 5, 0, 4)
     piece = jnp.roll(piece.reshape(2, 2 * BINS * W, SRC_BLOCK), -offset, axis=2)
-    sources = lax.all_gather(piece, ("chan", "band"), axis=0, tiled=True)
-
-    total = correlate(white, sources)
+    total = correlate(white, piece.reshape(PIECE, SRC_BLOCK))
     total = total.reshape(LAGS, own_rows, bands, SRC_BLOCK // bands).transpose(2, 3, 0, 1)
     total = lax.all_to_all(total, "band", split_axis=0, concat_axis=0, tiled=False)
     return total.transpose(1, 2, 0, 3).reshape(SRC_BLOCK // bands, LAGS, bands * own_rows)

time: 493 us -> 167 us (0.34)
  waiting for transfers between devices: 330 us -> 5.43 us
  Pallas kernels: 71.7 us -> 89 us
  between operations: 14.8 us -> 1.39 us
    all_gather x1 -> x0, waiting for transfers between devices: 325 us -> none  [body(): sources = lax.all_gather(piece, ('chan', 'band'), axis=0, tiled=True)]
    pallas_call x1, Pallas kernels: 56.4 us -> 73.8 us  [correlate(): pl.pallas_call(lag_kernel, in_specs=[anywhere] * 3, out_specs=pl.BlockSpe...]
  transfers between devices with their start and end apart: 2 -> 1, of which waited for: 2 -> 1; matrix products, arithmetic and copies ran while one was open for 0% -> 0% of each run, Pallas kernels for 0% -> 0%
where the time goes in v2:
time: 167 us; the launch traced here: 166 us
  Pallas kernels  89 us (53%)
  blocking collectives  53.6 us (32%)
  local copies, waits for them, and re-layouts  9.19 us (6%)
  waiting for transfers between devices  5.43 us (3%)
  starting transfers between devices  5.15 us (3%)
  other arithmetic  1.84 us (1%)
    pallas_call x1, Pallas kernels, correlate(): pl.pallas_call(lag_kernel, in_specs=[anywhere] * 3, out_specs=pl.BlockSpe...  73.8 us
    all_to_all x1, blocking collectives, body(): lax.all_to_all(masked, 'chan', split_axis=0, concat_axis=0, tiled=True)  36.2 us
    all_to_all x1, blocking collectives, body(): lax.all_to_all(total, 'band', split_axis=0, concat_axis=0, tiled=False)  17.4 us
    pallas_call x1, Pallas kernels, whiten(): pl.pallas_call(spectra_kernel, out_shape=(shape, shape), scratch_shapes=[...  15.3 us
    all_to_all x1, waiting for transfers between devices, body(): lax.all_to_all(piece, 'band', split_axis=0, concat_axis=0, tiled=True)  5.43 us
    all_to_all x1, starting transfers between devices, body(): lax.all_to_all(piece, 'band', split_axis=0, concat_axis=0, tiled=True)  5.15 us
  transfers between devices with their start and end apart: 1, of which 1 were waited for; matrix products, arithmetic and copies ran while one was open for 0% of the time, Pallas kernels for 0%

profile of v2, /device:TPU:1, one launch (start us, length us, event | category | flops | bytes accessed | tf_op | source)
XLA Modules:
  0.0 165.6 jit_solution(16739322882412556126)
XLA Ops:
  1.3 0.7 and_or_fusion
  2.0 0.1 and_convert_fusion
  2.1 0.1 reshape.74.mask
  2.1 0.8 copy-done
  3.0 0.7 copy-done.1
  3.7 0.7 copy-done.2
  4.4 0.7 copy-done.3
  5.1 15.3 %shard_map.91 = (bf16[32,128,256]{2,1,0:T(8,128)(2,1)S(1)}, bf16[32,128,256]{2,1,0:T(8,128)(2,1)S(1)}) custom-call(f32[16,34816]{1,0:T(8,128)} %strain.1, f32[32,128]{1,0:T(8,128)S(1)} %copy-done.3, f32[32,128]{1,0:T(8,128)S(1)} %copy-done.2, f32[32,128]{1,0:T(8,128)S(1)} %copy-done.1, bf16[128,256]{1,0:T(8,128)(2,1)S(1)} %copy-done, f32[1,256]{1,0:T(1,128)S(1)} %reshape.74.mask), custom_call_target="tpu_custom_call" | custom-call | flops 536870912 | bytes 8388608 | tf_op jit(solution)/shard_map/pallas_call | solution.py:143
  20.4 0.0 copy-start.4
  20.4 36.2 %all_to_all.15 = bf16[32,128,256]{2,1,0:T(8,128)(2,1)S(1)} all-to-all(bf16[32,128,256]{2,1,0:T(8,128)(2,1)S(1)} %get-tuple-element.8), channel_id=1, replica_groups=mesh['chan'=16,'band'=8] {'chan'}, dimensions={0} | all-to-all | bytes 4194304 | tf_op jit(solution)/shard_map/all_to_all | solution.py:405
  56.7 0.0 copy-done.4
  56.7 0.3 reduce_sum.12
  56.9 0.7 copy.19
  57.6 5.1 %all-to-all-start.1 = ((bf16[8,2,16,256]{3,2,1,0:T(8,128)(2,1)}), bf16[8,2,16,256]{3,2,1,0:T(8,128)(2,1)S(1)}, u32[]{:S(2)}, u32[]{:S(2)}) async-start(bf16[8,2,16,256]{3,2,1,0:T(8,128)(2,1)} %bitcast.6), calls=%async_computation.1 | async-start | bytes 262144 | tf_op jit(solution)/shard_map/all_to_all | solution.py:408
  62.8 5.4 %all-to-all-done.1 = bf16[8,2,16,256]{3,2,1,0:T(8,128)(2,1)S(1)} async-done(((bf16[8,2,16,256]{3,2,1,0:T(8,128)(2,1)}), bf16[8,2,16,256]{3,2,1,0:T(8,128)(2,1)S(1)}, u32[]{:S(2)}, u32[]{:S(2)}) %all-to-all-start.1) | async-done | bytes 131104 | tf_op jit(solution)/shard_map/all_to_all | solution.py:408
  68.2 0.7 reshape.69
  68.9 0.8 copy.20
  69.7 0.7 reshape.70
  70.4 0.8 fusion
  71.2 73.8 %shard_map.92 = bf16[256,2048]{1,0:T(8,128)(2,1)} custom-call(bf16[8,2,2,128,256]{4,3,2,1,0:T(8,128)(2,1)} %bitcast.25, bf16[512,128]{1,0:T(8,128)(2,1)} %bitcast.31, bf16[2,256,2048]{2,1,0:T(8,128)(2,1)} %constant.63.clone.tables), custom_call_target="tpu_custom_call" | custom-call | flops 8589934592 | bytes 20971520 | tf_op jit(solution)/shard_map/pallas_call | solution.py:367
  145.0 1.5 copy.21
  146.5 0.1 copy.22
  146.6 17.4 %all_to_all.16 = bf16[8,16,256,16]{2,1,3,0:T(8,128)(2,1)S(1)} all-to-all(bf16[8,16,256,16]{2,1,3,0:T(8,128)(2,1)S(1)} %copy.22), channel_id=1, replica_groups=mesh['chan'=16,'band'=8] {'band'}, dimensions={0} | all-to-all | bytes 2097152 | tf_op jit(solution)/shard_map/all_to_all | solution.py:413
  163.9 1.7 %copy.24 = bf16[16,256,128]{2,1,0:T(8,128)(2,1)} copy(bf16[16,256,128]{1,0,2:T(8,128)(2,1)S(1)} %bitcast.29) | data formatting | bytes 2097152 | tf_op jit(solution)/shard_map/reshape | solution.py:414
  (4 shorter events, 0.0 us)
Async XLA Ops:
  2.1 0.8 copy-start
  3.0 0.7 copy-start.1
  3.7 0.7 copy-start.2
  4.4 0.7 copy-start.3
  20.4 36.2 %copy-start.4 = (bf16[32,128,256]{2,1,0:T(8,128)(2,1)}, bf16[32,128,256]{2,1,0:T(8,128)(2,1)S(1)}, u32[]{:S(2)}) copy-start(bf16[32,128,256]{2,1,0:T(8,128)(2,1)S(1)} %get-tuple-element.7) | copy-start | bytes 6291460
  57.6 10.6 %all-to-all-start.1 = ((bf16[8,2,16,256]{3,2,1,0:T(8,128)(2,1)}), bf16[8,2,16,256]{3,2,1,0:T(8,128)(2,1)S(1)}, u32[]{:S(2)}, u32[]{:S(2)}) async-start(bf16[8,2,16,256]{3,2,1,0:T(8,128)(2,1)} %bitcast.6), calls=%async_computation.1 | async-start | bytes 262144 | tf_op jit(solution)/shard_map/all_to_all | solution.py:408

commit v3 on v2

v3 whole, which is shorter than its diff:
```python
import functools
import math

import jax
import jax.numpy as jnp
import numpy as np
from jax import lax
from jax.experimental import pallas as pl
from jax.experimental.pallas import tpu as pltpu
from jax.sharding import PartitionSpec as P

L = 4096
HOP = 2048
NF = 2048
W = 16
SRC_BLOCK = 128
LAGS = 256
R1 = 32
R2 = 128
HALF = R2 // 2
BINS = 8
FACTOR = 1.0 / (W * math.sqrt(NF))


def window_table():
    points = np.arange(L, dtype=np.float32)
    angle = (points * np.float32(2.0 * math.pi / L)).astype(np.float32)
    return (np.float32(0.5) - np.float32(0.5) * np.cos(angle)).astype(np.float32).reshape(R1, R2)


def row_tables():
    angle = 2.0 * np.pi * np.outer(np.arange(R1), np.arange(R2)) / L
    return np.concatenate([window_table(), np.cos(angle), -np.sin(angle)], axis=0).astype(np.float32)


def short_dft():
    angle = 2.0 * np.pi * (np.outer(np.arange(HALF), np.arange(R2)) % R2) / R2
    cosine, sine = np.cos(angle), np.sin(angle)
    top = np.concatenate([cosine, sine], axis=1)
    low = np.concatenate([-sine, cosine], axis=1)
    return np.concatenate([top, low], axis=0).astype(np.float32)


def lag_table():
    core, g, x, y_hi, y_lo, z_hi, z_lo, i = np.ix_(*[np.arange(n) for n in (2, 2, 4, 2, 2, 2, 2, 8)])
    bins = 8 * x + 4 * y_hi + 2 * core + y_lo + R1 * (16 * (2 * z_hi + z_lo) + 8 * g + i)
    lags = (np.arange(LAGS) - LAGS // 2).reshape((1, LAGS) + (1,) * 7)
    angle = 2.0 * np.pi * (lags * bins[:, None] % L) / L
    table = np.stack([np.cos(angle), -np.sin(angle)], axis=7)
    return table.reshape(2, LAGS, NF).astype(np.float32)


def real_dft(x):
    n = len(x)
    if n == 2:
        return [(x[0] + x[1], None), (x[0] - x[1], None)]
    even, odd = real_dft(x[0::2]), real_dft(x[1::2])
    out = [None] * (n // 2 + 1)
    for k in range(n // 4 + 1):
        er, ei = even[k]
        orr, oi = odd[k]
        if k == 0:
            out[0] = (er + orr, None)
            out[n // 2] = (er - orr, None)
            continue
        if 4 * k == n:
            out[k] = (er, -orr)
            continue
        c, s = math.cos(2 * math.pi * k / n), -math.sin(2 * math.pi * k / n)
        if oi is None:
            tr, ti = orr * c, orr * s
        else:
            tr, ti = orr * c - oi * s, orr * s + oi * c
        zi = ti if ei is None else ei + ti
        yi = -ti if ei is None else ei - ti
        out[k] = (er + tr, zi)
        out[n // 2 - k] = (er - tr, -yi)
    return out


SIDE = 4
SLOTS = SIDE ** 3
PIECE = 2 * 2 * BINS * W
PARTS = ((0, 48, 48, (0, 1, 2)), (96, 48, 32, (1, 2, 0)), (176, 32, 48, (2, 0, 1)))
ROUNDS = 2
MESH = pl.DeviceIdType.MESH


def position():
    chan, band = lax.axis_index("chan"), lax.axis_index("band")
    return (chan // 4, chan // 2 % 2 * 2 + band // 4, band % 4), chan % 2


def device_at(at, core):
    x, y, z = at
    return (x * 4 + y // 2 * 2 + core, y % 2 * 4 + z)


def neighbour(axis, step):
    at, core = position()
    moved = list(at)
    moved[axis] = lax.rem(at[axis] + step + SIDE, SIDE)
    return device_at(moved, core)


def slots(ref, at, full, first, count):
    whole = slice(None)
    x = whole if 0 in full else at[0]
    y_hi, y_lo = (whole, whole) if 1 in full else (at[1] // 2, at[1] % 2)
    z = whole if 2 in full else at[2]
    return ref.at[x, y_hi, y_lo, z, pl.ds(first, count), :]


def partners(at, core):
    x, y, z = at
    side = lambda step: lax.rem(z + step, SIDE)
    along = [((lax.rem(x + dx, SIDE), y ^ (2 * dy), z), core) for dx in range(SIDE) for dy in range(2)][1:]
    across = [((x, y ^ dy, side(dz)), core) for dy in range(2) for dz in range(SIDE)][1:]
    return along, across, [((x, y ^ 3, z), core), (at, 1 - core)]


def kernel(strain_hbm, rows_hbm, dft_hbm, tables, block, offset, valid, out,
           strain, rows, dft, table, held, mixed, parts, share, bands, spectra, left, cross, total,
           outgoing, incoming, turned, shipped, landed,
           local_sem, send_sem, recv_sem, side_send, side_recv, chan_send, chan_recv, band_send, band_recv,
           ship_send, ship_recv):
    at, core = position()
    chan, band = lax.axis_index("chan"), lax.axis_index("band")
    sibling = device_at(at, 1 - core)
    lanes = held.shape[-1]
    channels = lanes // W
    columns = channels * SRC_BLOCK
    along, across, rest = partners(at, core)

    def fetch(src, dst, index):
        copy = pltpu.make_async_copy(src, dst, local_sem.at[index])
        copy.start()
        return copy

    fetched = [fetch(strain_hbm, strain, 0), fetch(rows_hbm, rows, 1), fetch(dft_hbm, dft, 2)]
    own_table = fetch(tables.at[core], table, 3)
    barrier = pltpu.get_barrier_semaphore()
    for place, which in along + across + rest:
        pl.semaphore_signal(barrier, inc=1, device_id=device_at(place, which), device_id_type=MESH)
    for copy in fetched:
        copy.wait()

    folded = left.at[0]

    def fold(c, _):
        first = c // BINS * (BINS * (W + 1) * W) + c % BINS
        x = [strain[pl.ds(first + BINS * k, W, stride=BINS * W), :] for k in range(R1)]
        whole = x[0]
        for k in range(1, R1):
            whole = whole + x[k]
        mean = jnp.sum(whole, axis=1, keepdims=True) * (1.0 / L)
        x = [((x[k] - mean) * rows[k:k + 1, :]).astype(jnp.bfloat16).astype(jnp.float32) for k in range(R1)]
        bins = real_dft(x)
        to = pl.ds(pl.multiple_of(c * W, W), W)
        for f in range(R1):
            re, im = bins[f] if f <= R1 // 2 else bins[R1 - f]
            cosine, sine = rows[R1 + f:R1 + f + 1, :], rows[2 * R1 + f:2 * R1 + f + 1, :]
            if im is None:
                gr, gi = re * cosine, re * sine
            else:
                im = im if f <= R1 // 2 else -im
                gr, gi = re * cosine - im * sine, re * sine + im * cosine
            folded[f, to, :R2] = gr.astype(jnp.bfloat16)
            folded[f, to, R2:] = gi.astype(jnp.bfloat16)
        return 0

    lax.fori_loop(0, channels, fold, 0, unroll=2)
    dft_table = dft[...]

    def transform(f, power):
        y = lax.dot_general(dft_table, folded[f], (((1,), (1,)), ((), ())), preferred_element_type=jnp.float32)
        total[f, :R2, :] = y[:, :R2]
        total[f, R2:, :] = y[:, R2:]
        square = y * y
        return power + (square[:HALF] + square[HALF:])

    power = lax.fori_loop(0, R1, transform, jnp.zeros((HALF, lanes), jnp.float32), unroll=8)
    scales = []
    for b in range(HALF // BINS):
        mean = jnp.sum(power[b * BINS:(b + 1) * BINS], axis=0, keepdims=True) * (1.0 / 256.0)
        scales.append(jnp.broadcast_to(lax.rsqrt(mean + 1e-06), (BINS, lanes)))
    scale = jnp.concatenate(scales + scales, axis=0)

    def finish_white(to, which):
        def step(index, _):
            f = index // 2 * 4 + which * 2 + index % 2
            y = jnp.concatenate([total[f, :R2, :], total[f, R2:, :]], axis=1)
            held[to, index // 2, index % 2] = (y * scale).astype(jnp.bfloat16)
            return 0

        lax.fori_loop(0, R1 // 2, step, 0, unroll=4)

    finish_white(2, 1 - core)
    pl.semaphore_wait(barrier, len(along) + len(across) + len(rest))
    swap = pltpu.make_async_remote_copy(
        src_ref=held.at[2], dst_ref=held.at[1], send_sem=side_send.at[0], recv_sem=side_recv.at[0],
        device_id=sibling, device_id_type=MESH)
    swap.start()
    finish_white(0, core)

    row = lax.broadcasted_iota(jnp.int32, (2 * BINS, R2), 0) % BINS
    lane = lax.broadcasted_iota(jnp.int32, (2 * BINS, R2), 1)
    own = lane // W == row

    def spread(core_index):
        def step(index, _):
            x, y_hi, y_lo, z = index // 16, index // 8 % 2, index // 4 % 2, index % 4
            for ri in range(2):
                picked = pl.ds(pl.multiple_of(ri * HALF + z * 16, 16), 16)
                for k in range(channels // 8):
                    value = held[core_index, x * 2 + y_hi, y_lo, picked, k * R2:(k + 1) * R2].astype(jnp.float32)
                    for g in range(2):
                        even = pltpu.roll(value[g * BINS:(g + 1) * BINS], 0, 1, stride=W, stride_axis=0)
                        both = jnp.concatenate([even, pltpu.roll(even, R2 - W, 1)], axis=0)
                        for t in range(4):
                            moved = pltpu.roll(both, R2 - 2 * W * t, 1) if t else both
                            first = ((core_index * channels // 8 + k) * 4 + t) * 2 * BINS
                            left[g, index, first:first + 2 * BINS, ri * R2:(ri + 1) * R2] = jnp.where(
                                own, moved, 0.0).astype(jnp.bfloat16)
            return 0

        return step

    lax.fori_loop(0, 16, spread(0), 0)

    spot = lax.broadcasted_iota(jnp.int32, (1, lanes), 1)
    source = band * channels + spot // W
    stacked = jnp.zeros((1, lanes), jnp.float32)
    for w in range(W):
        stacked = jnp.where(spot % W == w, jnp.where(valid[w] != 0, 1.0, 0.0), stacked)
    chans = R1 // 2

    def chosen(which):
        first = jnp.where(which == block[0], 1, 0)
        second = jnp.where(which == lax.rem(block[0] + 1, chans), 1, 0)
        taken = jnp.where(source >= offset[0], first, second)
        return jnp.where(taken == 1, stacked, 0.0)

    mine, theirs = chosen(chan), chosen(chan ^ 1)
    swap.wait_recv()

    def mix(index, _):
        a, b = held[0, index // 2, index % 2], held[1, index // 2, index % 2]
        value = a.astype(jnp.float32) * mine + b.astype(jnp.float32) * theirs
        mixed[index // 2, index % 2] = value.astype(jnp.bfloat16)
        return 0

    lax.fori_loop(0, R1 // 2, mix, 0, unroll=4)
    slot = chan // 2
    sums = []
    for r, (place, which) in enumerate(along):
        target = place[0] * 2 + place[1] // 2
        sums.append(pltpu.make_async_remote_copy(
            src_ref=mixed.at[target], dst_ref=parts.at[slot], send_sem=chan_send.at[r], recv_sem=chan_recv.at[r],
            device_id=device_at(place, which), device_id_type=MESH))
    for copy in sums:
        copy.start()
    lax.fori_loop(16, SLOTS, spread(0), 0)
    lax.fori_loop(0, 24, spread(1), 0)
    for copy in sums:
        copy.wait_recv()
    parts[slot] = mixed[slot]
    for lo in range(2):
        value = parts[0, lo].astype(jnp.float32)
        for k in range(1, SIDE * 2):
            value = value + parts[k, lo].astype(jnp.float32)
        share[lo] = value.astype(jnp.bfloat16).reshape(2, SIDE, 16, lanes)

    moves = []
    for r, (place, which) in enumerate(across):
        moves.append(pltpu.make_async_remote_copy(
            src_ref=share.at[place[1] % 2, :, place[2]], dst_ref=bands.at[band],
            send_sem=band_send.at[r], recv_sem=band_recv.at[r],
            device_id=device_at(place, which), device_id_type=MESH))
    for copy in moves:
        copy.start()
    bands[band] = share[at[1] % 2, :, at[2]]
    lax.fori_loop(24, 40, spread(1), 0)
    for copy in moves:
        copy.wait_recv()

    wide = (BINS * W, lanes)
    same = lax.broadcasted_iota(jnp.int32, wide, 1) % W == lax.broadcasted_iota(jnp.int32, wide, 0) % W
    tall = (lanes, SRC_BLOCK)
    channel = lax.broadcasted_iota(jnp.int32, tall, 0) // W
    column = lax.broadcasted_iota(jnp.int32, tall, 1)
    value = None
    for b in range(2 * SIDE):
        goal = (channel + (b * channels + SRC_BLOCK) - offset[0]) % SRC_BLOCK
        pick = jnp.where(goal == column, 1.0, 0.0).astype(jnp.bfloat16)
        blocks = []
        for g in range(2):
            for ri in range(2):
                part = bands[b, ri].astype(jnp.float32)[g * BINS:(g + 1) * BINS]
                part = jnp.broadcast_to(part[:, None, :], (BINS, W, lanes)).reshape(wide)
                blocks.append(jnp.where(same, part, 0.0).astype(jnp.bfloat16))
        term = jnp.dot(jnp.concatenate(blocks, axis=0), pick, preferred_element_type=jnp.float32)
        value = term if value is None else value + term
    spectra[at[0], at[1] // 2, at[1] % 2, at[2]] = value.astype(jnp.bfloat16)

    copies = {}

    def start(turn, stage, part, kind):
        first, low, high, order = PARTS[part]
        first += turn * (PIECE // ROUNDS)
        axis, full = order[stage], order[:stage]
        if kind < 2:
            ref = slots(spectra, at, full, first, low + high)
        else:
            moved = list(at)
            moved[axis] = lax.rem(at[axis] + (SIDE - 1 if kind == 2 else 1), SIDE)
            ref = slots(spectra, moved, full, first + (0 if kind == 2 else low), low if kind == 2 else high)
        index = ((turn * 3 + stage) * 3 + part) * 4 + kind
        copy = pltpu.make_async_remote_copy(
            src_ref=ref, dst_ref=ref, send_sem=send_sem.at[index], recv_sem=recv_sem.at[index],
            device_id=neighbour(axis, 1 if kind % 2 == 0 else -1), device_id_type=MESH)
        copies[turn, stage, part, kind] = copy
        copy.start()

    def begin(turn, stage):
        for part in range(3):
            start(turn, stage, part, 0)
            start(turn, stage, part, 1)

    def forward(turn, stage):
        for part in range(3):
            copies[turn, stage, part, 0].wait_recv()
            start(turn, stage, part, 2)
            copies[turn, stage, part, 1].wait_recv()
            start(turn, stage, part, 3)

    def finish(turn, stage):
        for part in range(3):
            copies[turn, stage, part, 2].wait_recv()
            copies[turn, stage, part, 3].wait_recv()

    def multiply(turn):
        def step(index, _):
            results = []
            for h in range(2):
                k = index * 2 + h
                s = spectra[k // 16, k // 8 % 2, k // 4 % 2, k % 4, turn * 256:(turn + 1) * 256, :]
                right = jnp.concatenate([s, jnp.concatenate([-s[R2:], s[:R2]], axis=0)], axis=1)
                results.append(jnp.dot(left[turn, k], right, preferred_element_type=jnp.float32))
            base = pl.multiple_of(index * 32, 32)
            for c in range(2 * channels):
                both = jnp.concatenate([r[c * BINS:(c + 1) * BINS] for r in results], axis=0).astype(jnp.bfloat16)
                cross[pl.ds(base, 16), c * SRC_BLOCK:(c + 1) * SRC_BLOCK] = both[:, :SRC_BLOCK]
                cross[pl.ds(base + 16, 16), c * SRC_BLOCK:(c + 1) * SRC_BLOCK] = both[:, SRC_BLOCK:]
            return 0

        return step

    group = 8
    width = group * SRC_BLOCK

    def sum_lags(turn, core_index, store):
        def step(n, _):
            both = pl.ds(pl.multiple_of(core_index * columns + n * width, width), width)
            value = jnp.dot(table[:, turn * 1024:(turn + 1) * 1024], cross[:, both],
                            preferred_element_type=jnp.float32)
            for i in range(group):
                store(n * group + i, core_index * channels + n * group + i,
                      value[:, i * SRC_BLOCK:(i + 1) * SRC_BLOCK])
            return 0

        lax.fori_loop(0, channels // group, step, 0)

    def keep(c, held_c, value):
        total[held_c] = value

    def hand_over(c, held_c, value):
        outgoing[c] = ((total[held_c] + value) * FACTOR).astype(jnp.bfloat16)

    def conclude(c, held_c, value):
        total[held_c] = total[held_c] + value

    pairs = SLOTS // 2
    begin(0, 0)
    lax.fori_loop(40, 48, spread(1), 0)
    forward(0, 0)
    finish(0, 0)
    begin(0, 1)
    begin(1, 0)
    lax.fori_loop(48, 56, spread(1), 0)
    forward(0, 1)
    forward(1, 0)
    lax.fori_loop(56, 60, spread(1), 0)
    finish(0, 1)
    finish(1, 0)
    begin(0, 2)
    begin(1, 1)
    lax.fori_loop(60, SLOTS, spread(1), 0)
    forward(1, 1)
    forward(0, 2)
    finish(1, 1)
    finish(0, 2)
    begin(1, 2)
    own_table.wait()
    lax.fori_loop(0, pairs, multiply(0), 0, unroll=2)
    forward(1, 2)
    sum_lags(0, 0, keep)
    sum_lags(0, 1, keep)
    finish(1, 2)
    lax.fori_loop(0, pairs, multiply(1), 0, unroll=2)
    sum_lags(1, 1, hand_over)
    exchange = pltpu.make_async_remote_copy(
        src_ref=outgoing, dst_ref=incoming, send_sem=side_send.at[1], recv_sem=side_recv.at[1],
        device_id=sibling, device_id_type=MESH)
    exchange.start()
    sum_lags(1, 0, conclude)
    exchange.wait_recv()

    diagonal = (lax.broadcasted_iota(jnp.int32, (LAGS, LAGS), 0) == lax.broadcasted_iota(jnp.int32, (LAGS, LAGS), 1))
    unit = jnp.where(diagonal, 1.0, 0.0).astype(jnp.bfloat16)
    last = (((1,), (1,)), ((), ()))
    for c in range(channels):
        value = (total[c] * FACTOR + incoming[c].astype(jnp.float32)).astype(jnp.bfloat16)
        value = lax.dot_general(unit[:SRC_BLOCK, :SRC_BLOCK], value, last, preferred_element_type=jnp.float32)
        for half in range(2):
            turned[half, pl.ds(c, SRC_BLOCK, stride=channels), :] = value[:, half * R2:(half + 1) * R2]

    def pack(index):
        picked = pl.ds(pl.multiple_of(index * 256, 256), 256)
        return jnp.concatenate([turned[0, picked, :], turned[1, picked, :]], axis=1).astype(jnp.bfloat16)

    ships = []
    for r, (place, which) in enumerate(across):
        index = place[1] % 2 * SIDE + place[2]
        shipped[index] = pack(index)
        ship = pltpu.make_async_remote_copy(
            src_ref=shipped.at[index], dst_ref=landed.at[band], send_sem=ship_send.at[r], recv_sem=ship_recv.at[r],
            device_id=device_at(place, which), device_id_type=MESH)
        ship.start()
        ships.append(ship)
    landed[band] = pack(band)
    for ship in ships:
        ship.wait_recv()
    for s in range(SRC_BLOCK // (2 * SIDE)):
        value = landed[:, s * channels:(s + 1) * channels, :].reshape(2 * SIDE * channels, LAGS)
        out[s] = lax.dot_general(unit, value, last, preferred_element_type=jnp.float32).astype(out.dtype)

    for copy in [swap, exchange] + sums + moves + ships + list(copies.values()):
        copy.wait_send()


def body(strain, source_block, source_offset, window_valid):
    channels = strain.shape[0]
    lanes = channels * W
    columns = channels * SRC_BLOCK
    tiles = strain.reshape(channels // BINS, BINS, -1, R2).transpose(0, 2, 1, 3).reshape(-1, R2)
    copies = ROUNDS * 3 * 3 * 4
    anywhere = pl.BlockSpec(memory_space=pl.ANY)
    scalars = pl.BlockSpec(memory_space=pltpu.SMEM)
    dma = pltpu.SemaphoreType.DMA
    bf16, f32 = jnp.bfloat16, jnp.float32
    return pl.pallas_call(
        kernel,
        in_specs=[anywhere] * 4 + [scalars] * 3,
        out_specs=pl.BlockSpec(memory_space=pltpu.VMEM),
        out_shape=jax.ShapeDtypeStruct((SRC_BLOCK // (2 * SIDE), LAGS, 2 * SIDE * channels), bf16),
        scratch_shapes=[
            pltpu.VMEM(tiles.shape, f32),
            pltpu.VMEM((3 * R1, R2), f32),
            pltpu.VMEM((R2, 2 * R2), bf16),
            pltpu.VMEM((LAGS, NF), bf16),
            pltpu.VMEM((3, SIDE * 2, 2, R2, lanes), bf16),
            pltpu.VMEM((SIDE * 2, 2, R2, lanes), bf16),
            pltpu.VMEM((SIDE * 2, 2, R2, lanes), bf16),
            pltpu.VMEM((2, 2, SIDE, 16, lanes), bf16),
            pltpu.VMEM((2 * SIDE, 2, 16, lanes), bf16),
            pltpu.VMEM((SIDE, 2, 2, SIDE, PIECE, SRC_BLOCK), bf16),
            pltpu.VMEM((2, SLOTS, 256, 256), bf16),
            pltpu.VMEM((NF // 2, 2 * columns), bf16),
            pltpu.VMEM((2 * channels, LAGS, SRC_BLOCK), f32),
            pltpu.VMEM((channels, LAGS, SRC_BLOCK), bf16),
            pltpu.VMEM((channels, LAGS, SRC_BLOCK), bf16),
            pltpu.VMEM((2, columns, R2), f32),
            pltpu.VMEM((2 * SIDE, 256, LAGS), bf16),
            pltpu.VMEM((2 * SIDE, 256, LAGS), bf16),
            dma((4,)), dma((copies,)), dma((copies,)), dma((2,)), dma((2,)),
            dma((7,)), dma((7,)), dma((7,)), dma((7,)), dma((7,)), dma((7,)),
        ],
        compiler_params=pltpu.CompilerParams(
            vmem_limit_bytes=62 * 2**20, collective_id=1, has_side_effects=True),
        cost_estimate=pl.CostEstimate(flops=4 * 256 * 4096 * 2048, bytes_accessed=20 * 2**20, transcendentals=0),
    )(tiles, jnp.asarray(row_tables()), jnp.asarray(short_dft(), dtype=bf16),
      jnp.asarray(lag_table(), dtype=bf16), source_block, source_offset, window_valid)


def solution(mesh):
    in_specs = (P(("chan", "band"), None), P(), P(), P())
    out_specs = P("band", None, "chan")
    return jax.shard_map(body, mesh=mesh, in_specs=in_specs, out_specs=out_specs, check_vma=False)
```

time: 167 us -> 124 us (0.74)
  blocking collectives: 53.6 us -> 0 us
  Pallas kernels: 89 us -> 120 us
  local copies, waits for them, and re-layouts: 9.19 us -> 2.3 us
  waiting for transfers between devices: 5.43 us -> 0 us
  starting transfers between devices: 5.15 us -> 0 us
  other arithmetic: 1.84 us -> 0 us
    all_to_all x2 -> x0, blocking collectives: 53.6 us -> none  [the longest x1 36.2 us: body(): lax.all_to_all(masked, 'chan', split_axis=0, concat_axis=0, tiled=True)]
    pallas_call x2 -> x1, Pallas kernels: 89 us -> 120 us  [body(): pl.pallas_call(kernel, in_specs=[anywhere] * 4 + [scalars] * 3, out_specs...]
    all_to_all x1 -> x0, waiting for transfers between devices: 5.43 us -> none  [body(): lax.all_to_all(piece, 'band', split_axis=0, concat_axis=0, tiled=True)]
    all_to_all x1 -> x0, starting transfers between devices: 5.15 us -> none  [body(): lax.all_to_all(piece, 'band', split_axis=0, concat_axis=0, tiled=True)]
    reshape x3 -> x0, local copies, waits for them, and re-layouts: 3.07 us -> none  [the longest x1 1.69 us: body(): total.transpose(1, 2, 0, 3)]
  transfers between devices with their start and end apart: 1 -> 0, of which waited for: 1 -> 0; matrix products, arithmetic and copies ran while one was open for 0% -> 0% of each run, Pallas kernels for 0% -> 0%
where the time goes in v3:
time: 124 us
  Pallas kernels  120 us (97%)
  local copies, waits for them, and re-layouts  2.3 us (2%)
  between operations  1.3 us (1%)
    pallas_call x1, Pallas kernels, body(): pl.pallas_call(kernel, in_specs=[anywhere] * 4 + [scalars] * 3, out_specs...  120 us

profile of v3, /device:TPU:1, one launch (start us, length us, event | category | flops | bytes accessed | tf_op | source)
XLA Modules:
  0.0 124.0 jit_solution(13932640176761286036)
XLA Ops:
  1.3 120.4 %shard_map.73 = bf16[16,256,128]{2,1,0:T(8,128)(2,1)} custom-call(f32[4352,128]{1,0:T(8,128)} %bitcast.5, f32[96,128]{1,0:T(8,128)} %constant.6.clone.rows_hbm, bf16[128,256]{1,0:T(8,128)(2,1)} %constant.7.clone.dft_hbm, bf16[2,256,2048]{2,1,0:T(8,128)(2,1)} %constant.8.clone.tables, s32[1]{0:T(128)S(6)} %copy.9.block, s32[1]{0:T(128)S(6)} %copy.10.offset, ...), custom_call_target="tpu_custom_call" | custom-call | flops 8589934592 | bytes 20971520 | tf_op jit(solution)/shard_map/pallas_call | solution.py:462
  121.7 2.3 %copy.11 = bf16[16,256,128]{2,1,0:T(8,128)(2,1)} copy(bf16[16,256,128]{2,1,0:T(8,128)(2,1)} %shard_map.73) | data formatting | bytes 2097152

commit v4 on v3

--- a/solution.py
+++ b/solution.py
@@ -38,12 +38,13 @@
     cosine, sine = np.cos(angle), np.sin(angle)
     top = np.concatenate([cosine, sine], axis=1)
     low = np.concatenate([-sine, cosine], axis=1)
-    return np.concatenate([top, low], axis=0).astype(np.float32)
+    both = np.stack([top.reshape(-1, BINS, 2 * R2), low.reshape(-1, BINS, 2 * R2)], axis=1)
+    return both.reshape(R2, 2 * R2).astype(np.float32)
 
 
 def lag_table():
     core, g, x, y_hi, y_lo, z_hi, z_lo, i = np.ix_(*[np.arange(n) for n in (2, 2, 4, 2, 2, 2, 2, 8)])
-    bins = 8 * x + 4 * y_hi + 2 * core + y_lo + R1 * (16 * (2 * z_hi + z_lo) + 8 * g + i)
+    bins = 8 * x + 4 * y_hi + 2 * core + g + R1 * (32 * y_lo + 8 * (2 * z_hi + z_lo) + i)
     lags = (np.arange(LAGS) - LAGS // 2).reshape((1, LAGS) + (1,) * 7)
     angle = 2.0 * np.pi * (lags * bins[:, None] % L) / L
     table = np.stack([np.cos(angle), -np.sin(angle)], axis=7)
@@ -114,8 +115,8 @@
 def partners(at, core):
     x, y, z = at
     side = lambda step: lax.rem(z + step, SIDE)
-    along = [((lax.rem(x + dx, SIDE), y ^ (2 * dy), z), core) for dx in range(SIDE) for dy in range(2)][1:]
-    across = [((x, y ^ dy, side(dz)), core) for dy in range(2) for dz in range(SIDE)][1:]
+    along = [((lax.rem(x + dx, SIDE), y ^ (2 * dy), z), core) for dx in (2, 1, 3, 0) for dy in (1, 0)][:-1]
+    across = [((x, y ^ dy, side(dz)), core) for dz in (2, 1, 3, 0) for dy in (1, 0)][:-1]
     return along, across, [((x, y ^ 3, z), core), (at, 1 - core)]
 
 
@@ -176,32 +177,37 @@
         y = lax.dot_general(dft_table, folded[f], (((1,), (1,)), ((), ())), preferred_element_type=jnp.float32)
         total[f, :R2, :] = y[:, :R2]
         total[f, R2:, :] = y[:, R2:]
-        square = y * y
-        return power + (square[:HALF] + square[HALF:])
+        square = (y * y).reshape(HALF // BINS, 2, BINS, lanes)
+        return power + (square[:, 0] + square[:, 1]).reshape(HALF, lanes)
 
     power = lax.fori_loop(0, R1, transform, jnp.zeros((HALF, lanes), jnp.float32), unroll=8)
     scales = []
     for b in range(HALF // BINS):
         mean = jnp.sum(power[b * BINS:(b + 1) * BINS], axis=0, keepdims=True) * (1.0 / 256.0)
-        scales.append(jnp.broadcast_to(lax.rsqrt(mean + 1e-06), (BINS, lanes)))
-    scale = jnp.concatenate(scales + scales, axis=0)
-
-    def finish_white(to, which):
+        scales.append(jnp.broadcast_to(lax.rsqrt(mean + 1e-06), (2 * BINS, lanes)))
+    scale = jnp.concatenate(scales, axis=0)
+
+    def finish_white(to, which, g):
         def step(index, _):
-            f = index // 2 * 4 + which * 2 + index % 2
+            f = index * 4 + which * 2 + g
             y = jnp.concatenate([total[f, :R2, :], total[f, R2:, :]], axis=1)
-            held[to, index // 2, index % 2] = (y * scale).astype(jnp.bfloat16)
+            held[to, g, index] = (y * scale).astype(jnp.bfloat16)
             return 0
 
-        lax.fori_loop(0, R1 // 2, step, 0, unroll=4)
-
-    finish_white(2, 1 - core)
+        lax.fori_loop(0, SIDE * 2, step, 0, unroll=4)
+
+    for g in range(2):
+        finish_white(2, 1 - core, g)
     pl.semaphore_wait(barrier, len(along) + len(across) + len(rest))
-    swap = pltpu.make_async_remote_copy(
-        src_ref=held.at[2], dst_ref=held.at[1], send_sem=side_send.at[0], recv_sem=side_recv.at[0],
-        device_id=sibling, device_id_type=MESH)
-    swap.start()
-    finish_white(0, core)
+    swaps = []
+    for g in range(2):
+        swap = pltpu.make_async_remote_copy(
+            src_ref=held.at[2, g], dst_ref=held.at[1, g], send_sem=side_send.at[g], recv_sem=side_recv.at[g],
+            device_id=sibling, device_id_type=MESH)
+        swap.start()
+        swaps.append(swap)
+    for g in range(2):
+        finish_white(0, core, g)
 
     row = lax.broadcasted_iota(jnp.int32, (2 * BINS, R2), 0) % BINS
     lane = lax.broadcasted_iota(jnp.int32, (2 * BINS, R2), 1)
@@ -210,12 +216,12 @@
     def spread(core_index):
         def step(index, _):
             x, y_hi, y_lo, z = index // 16, index // 8 % 2, index // 4 % 2, index % 4
-            for ri in range(2):
-                picked = pl.ds(pl.multiple_of(ri * HALF + z * 16, 16), 16)
+            picked = pl.ds(pl.multiple_of((y_lo * SIDE + z) * 16, 16), 16)
+            for g in range(2):
                 for k in range(channels // 8):
-                    value = held[core_index, x * 2 + y_hi, y_lo, picked, k * R2:(k + 1) * R2].astype(jnp.float32)
-                    for g in range(2):
-                        even = pltpu.roll(value[g * BINS:(g + 1) * BINS], 0, 1, stride=W, stride_axis=0)
+                    value = held[core_index, g, x * 2 + y_hi, picked, k * R2:(k + 1) * R2].astype(jnp.float32)
+                    for ri in range(2):
+                        even = pltpu.roll(value[ri * BINS:(ri + 1) * BINS], 0, 1, stride=W, stride_axis=0)
                         both = jnp.concatenate([even, pltpu.roll(even, R2 - W, 1)], axis=0)
                         for t in range(4):
                             moved = pltpu.roll(both, R2 - 2 * W * t, 1) if t else both
@@ -226,7 +232,7 @@
 
         return step
 
-    lax.fori_loop(0, 16, spread(0), 0)
+    lax.fori_loop(0, 8, spread(0), 0)
 
     spot = lax.broadcasted_iota(jnp.int32, (1, lanes), 1)
     source = band * channels + spot // W
@@ -242,66 +248,67 @@
         return jnp.where(taken == 1, stacked, 0.0)
 
     mine, theirs = chosen(chan), chosen(chan ^ 1)
-    swap.wait_recv()
-
-    def mix(index, _):
-        a, b = held[0, index // 2, index % 2], held[1, index // 2, index % 2]
-        value = a.astype(jnp.float32) * mine + b.astype(jnp.float32) * theirs
-        mixed[index // 2, index % 2] = value.astype(jnp.bfloat16)
-        return 0
-
-    lax.fori_loop(0, R1 // 2, mix, 0, unroll=4)
     slot = chan // 2
-    sums = []
-    for r, (place, which) in enumerate(along):
-        target = place[0] * 2 + place[1] // 2
-        sums.append(pltpu.make_async_remote_copy(
-            src_ref=mixed.at[target], dst_ref=parts.at[slot], send_sem=chan_send.at[r], recv_sem=chan_recv.at[r],
-            device_id=device_at(place, which), device_id_type=MESH))
-    for copy in sums:
-        copy.start()
-    lax.fori_loop(16, SLOTS, spread(0), 0)
-    lax.fori_loop(0, 24, spread(1), 0)
-    for copy in sums:
-        copy.wait_recv()
-    parts[slot] = mixed[slot]
-    for lo in range(2):
-        value = parts[0, lo].astype(jnp.float32)
+
+    def mix(g):
+        def step(index, _):
+            a, b = held[0, g, index], held[1, g, index]
+            value = a.astype(jnp.float32) * mine + b.astype(jnp.float32) * theirs
+            mixed[g, index] = value.astype(jnp.bfloat16)
+            return 0
+
+        return step
+
+    sums, moves = {}, {}
+    for g in range(2):
+        swaps[g].wait_recv()
+        lax.fori_loop(0, SIDE * 2, mix(g), 0, unroll=4)
+        sums[g] = []
+        for r, (place, which) in enumerate(along):
+            target = place[0] * 2 + place[1] // 2
+            sums[g].append(pltpu.make_async_remote_copy(
+                src_ref=mixed.at[g, target], dst_ref=parts.at[g, slot],
+                send_sem=chan_send.at[g * 7 + r], recv_sem=chan_recv.at[g * 7 + r],
+                device_id=device_at(place, which), device_id_type=MESH))
+        for copy in sums[g]:
+            copy.start()
+
+    def to_bands(g):
+        for copy in sums[g]:
+            copy.wait_recv()
+        parts[g, slot] = mixed[g, slot]
+        value = parts[g, 0].astype(jnp.float32)
         for k in range(1, SIDE * 2):
-            value = value + parts[k, lo].astype(jnp.float32)
-        share[lo] = value.astype(jnp.bfloat16).reshape(2, SIDE, 16, lanes)
-
-    moves = []
-    for r, (place, which) in enumerate(across):
-        moves.append(pltpu.make_async_remote_copy(
-            src_ref=share.at[place[1] % 2, :, place[2]], dst_ref=bands.at[band],
-            send_sem=band_send.at[r], recv_sem=band_recv.at[r],
-            device_id=device_at(place, which), device_id_type=MESH))
-    for copy in moves:
-        copy.start()
-    bands[band] = share[at[1] % 2, :, at[2]]
-    lax.fori_loop(24, 40, spread(1), 0)
-    for copy in moves:
-        copy.wait_recv()
-
-    wide = (BINS * W, lanes)
-    same = lax.broadcasted_iota(jnp.int32, wide, 1) % W == lax.broadcasted_iota(jnp.int32, wide, 0) % W
-    tall = (lanes, SRC_BLOCK)
-    channel = lax.broadcasted_iota(jnp.int32, tall, 0) // W
-    column = lax.broadcasted_iota(jnp.int32, tall, 1)
-    value = None
-    for b in range(2 * SIDE):
-        goal = (channel + (b * channels + SRC_BLOCK) - offset[0]) % SRC_BLOCK
-        pick = jnp.where(goal == column, 1.0, 0.0).astype(jnp.bfloat16)
-        blocks = []
-        for g in range(2):
-            for ri in range(2):
-                part = bands[b, ri].astype(jnp.float32)[g * BINS:(g + 1) * BINS]
-                part = jnp.broadcast_to(part[:, None, :], (BINS, W, lanes)).reshape(wide)
-                blocks.append(jnp.where(same, part, 0.0).astype(jnp.bfloat16))
-        term = jnp.dot(jnp.concatenate(blocks, axis=0), pick, preferred_element_type=jnp.float32)
-        value = term if value is None else value + term
-    spectra[at[0], at[1] // 2, at[1] % 2, at[2]] = value.astype(jnp.bfloat16)
+            value = value + parts[g, k].astype(jnp.float32)
+        share[g] = value.astype(jnp.bfloat16).reshape(2 * SIDE, 2 * BINS, lanes)
+        moves[g] = []
+        for r, (place, which) in enumerate(across):
+            moves[g].append(pltpu.make_async_remote_copy(
+                src_ref=share.at[g, place[1] % 2 * SIDE + place[2]], dst_ref=bands.at[g, band],
+                send_sem=band_send.at[g * 7 + r], recv_sem=band_recv.at[g * 7 + r],
+                device_id=device_at(place, which), device_id_type=MESH))
+        for copy in moves[g]:
+            copy.start()
+        bands[g, band] = share[g, band]
+
+    def arrange(g):
+        for copy in moves[g]:
+            copy.wait_recv()
+        wide = (2 * BINS * W, lanes)
+        same = lax.broadcasted_iota(jnp.int32, wide, 1) % W == lax.broadcasted_iota(jnp.int32, wide, 0) % W
+        tall = (lanes, SRC_BLOCK)
+        channel = lax.broadcasted_iota(jnp.int32, tall, 0) // W
+        column = lax.broadcasted_iota(jnp.int32, tall, 1)
+        value = None
+        for b in range(2 * SIDE):
+            goal = (channel + (b * channels + SRC_BLOCK) - offset[0]) % SRC_BLOCK
+            pick = jnp.where(goal == column, 1.0, 0.0).astype(jnp.bfloat16)
+            part = bands[g, b].astype(jnp.float32)
+            part = jnp.broadcast_to(part[:, None, :], (2 * BINS, W, lanes)).reshape(wide)
+            part = jnp.where(same, part, 0.0).astype(jnp.bfloat16)
+            term = jnp.dot(part, pick, preferred_element_type=jnp.float32)
+            value = term if value is None else value + term
+        spectra[at[0], at[1] // 2, at[1] % 2, at[2], g * wide[0]:(g + 1) * wide[0], :] = value.astype(jnp.bfloat16)
 
     copies = {}
 
@@ -309,7 +316,7 @@
         first, low, high, order = PARTS[part]
         first += turn * (PIECE // ROUNDS)
         axis, full = order[stage], order[:stage]
-        if kind < 2:
+        if kind < 2 or stage < 2:
             ref = slots(spectra, at, full, first, low + high)
         else:
             moved = list(at)
@@ -318,7 +325,8 @@
         index = ((turn * 3 + stage) * 3 + part) * 4 + kind
         copy = pltpu.make_async_remote_copy(
             src_ref=ref, dst_ref=ref, send_sem=send_sem.at[index], recv_sem=recv_sem.at[index],
-            device_id=neighbour(axis, 1 if kind % 2 == 0 else -1), device_id_type=MESH)
+            device_id=neighbour(axis, 2 if kind == 2 and stage < 2 else 1 if kind % 2 == 0 else -1),
+            device_id_type=MESH)
         copies[turn, stage, part, kind] = copy
         copy.start()
 
@@ -326,6 +334,8 @@
         for part in range(3):
             start(turn, stage, part, 0)
             start(turn, stage, part, 1)
+            if stage < 2:
+                start(turn, stage, part, 2)
 
     def forward(turn, stage):
         for part in range(3):
@@ -336,8 +346,8 @@
 
     def finish(turn, stage):
         for part in range(3):
-            copies[turn, stage, part, 2].wait_recv()
-            copies[turn, stage, part, 3].wait_recv()
+            for kind in (2, 3) if stage == 2 else (0, 1, 2):
+                copies[turn, stage, part, kind].wait_recv()
 
     def multiply(turn):
         def step(index, _):
@@ -381,26 +391,27 @@
         total[held_c] = total[held_c] + value
 
     pairs = SLOTS // 2
+    lax.fori_loop(8, SLOTS, spread(0), 0)
+    to_bands(0)
+    lax.fori_loop(0, 24, spread(1), 0)
+    arrange(0)
     begin(0, 0)
-    lax.fori_loop(40, 48, spread(1), 0)
-    forward(0, 0)
+    to_bands(1)
+    lax.fori_loop(24, 36, spread(1), 0)
     finish(0, 0)
     begin(0, 1)
+    arrange(1)
     begin(1, 0)
-    lax.fori_loop(48, 56, spread(1), 0)
-    forward(0, 1)
-    forward(1, 0)
-    lax.fori_loop(56, 60, spread(1), 0)
+    lax.fori_loop(36, 56, spread(1), 0)
     finish(0, 1)
+    begin(0, 2)
     finish(1, 0)
-    begin(0, 2)
     begin(1, 1)
-    lax.fori_loop(60, SLOTS, spread(1), 0)
-    forward(1, 1)
+    lax.fori_loop(56, SLOTS, spread(1), 0)
     forward(0, 2)
     finish(1, 1)
+    begin(1, 2)
     finish(0, 2)
-    begin(1, 2)
     own_table.wait()
     lax.fori_loop(0, pairs, multiply(0), 0, unroll=2)
     forward(1, 2)
@@ -410,7 +421,7 @@
     lax.fori_loop(0, pairs, multiply(1), 0, unroll=2)
     sum_lags(1, 1, hand_over)
     exchange = pltpu.make_async_remote_copy(
-        src_ref=outgoing, dst_ref=incoming, send_sem=side_send.at[1], recv_sem=side_recv.at[1],
+        src_ref=outgoing, dst_ref=incoming, send_sem=side_send.at[2], recv_sem=side_recv.at[2],
         device_id=sibling, device_id_type=MESH)
     exchange.start()
     sum_lags(1, 0, conclude)
@@ -445,7 +456,7 @@
         value = landed[:, s * channels:(s + 1) * channels, :].reshape(2 * SIDE * channels, LAGS)
         out[s] = lax.dot_general(unit, value, last, preferred_element_type=jnp.float32).astype(out.dtype)
 
-    for copy in [swap, exchange] + sums + moves + ships + list(copies.values()):
+    for copy in swaps + [exchange] + sums[0] + sums[1] + moves[0] + moves[1] + ships + list(copies.values()):
         copy.wait_send()
 
 
@@ -469,11 +480,11 @@
             pltpu.VMEM((3 * R1, R2), f32),
             pltpu.VMEM((R2, 2 * R2), bf16),
             pltpu.VMEM((LAGS, NF), bf16),
-            pltpu.VMEM((3, SIDE * 2, 2, R2, lanes), bf16),
-            pltpu.VMEM((SIDE * 2, 2, R2, lanes), bf16),
-            pltpu.VMEM((SIDE * 2, 2, R2, lanes), bf16),
-            pltpu.VMEM((2, 2, SIDE, 16, lanes), bf16),
-            pltpu.VMEM((2 * SIDE, 2, 16, lanes), bf16),
+            pltpu.VMEM((3, 2, SIDE * 2, R2, lanes), bf16),
+            pltpu.VMEM((2, SIDE * 2, R2, lanes), bf16),
+            pltpu.VMEM((2, SIDE * 2, R2, lanes), bf16),
+            pltpu.VMEM((2, SIDE * 2, 2 * BINS, lanes), bf16),
+            pltpu.VMEM((2, SIDE * 2, 2 * BINS, lanes), bf16),
             pltpu.VMEM((SIDE, 2, 2, SIDE, PIECE, SRC_BLOCK), bf16),
             pltpu.VMEM((2, SLOTS, 256, 256), bf16),
             pltpu.VMEM((NF // 2, 2 * columns), bf16),
@@ -483,8 +494,8 @@
             pltpu.VMEM((2, columns, R2), f32),
             pltpu.VMEM((2 * SIDE, 256, LAGS), bf16),
             pltpu.VMEM((2 * SIDE, 256, LAGS), bf16),
-            dma((4,)), dma((copies,)), dma((copies,)), dma((2,)), dma((2,)),
-            dma((7,)), dma((7,)), dma((7,)), dma((7,)), dma((7,)), dma((7,)),
+            dma((4,)), dma((copies,)), dma((copies,)), dma((3,)), dma((3,)),
+            dma((14,)), dma((14,)), dma((14,)), dma((14,)), dma((7,)), dma((7,)),
         ],
         compiler_params=pltpu.CompilerParams(
             vmem_limit_bytes=62 * 2**20, collective_id=1, has_side_effects=True),

time: 124 us -> 112 us (0.903)
  Pallas kernels: 120 us -> 109 us
    pallas_call x1, Pallas kernels: 120 us -> 109 us  [body(): pl.pallas_call(kernel, in_specs=[anywhere] * 4 + [scalars] * 3, out_specs...]
where the time goes in v4:
time: 112 us
  Pallas kernels  109 us (97%)
  local copies, waits for them, and re-layouts  2.3 us (2%)
  between operations  1.3 us (1%)
    pallas_call x1, Pallas kernels, body(): pl.pallas_call(kernel, in_specs=[anywhere] * 4 + [scalars] * 3, out_specs...  109 us
    unnamed x1, local copies, waits for them, and re-layouts  2.3 us

profile of v4, /device:TPU:1, one launch (start us, length us, event | category | flops | bytes accessed | tf_op | source)
XLA Modules:
  0.0 112.1 jit_solution(10864861687249986818)
XLA Ops:
  1.3 108.5 %shard_map.73 = bf16[16,256,128]{2,1,0:T(8,128)(2,1)} custom-call(f32[4352,128]{1,0:T(8,128)} %bitcast.5, f32[96,128]{1,0:T(8,128)} %constant.6.clone.rows_hbm, bf16[128,256]{1,0:T(8,128)(2,1)} %constant.7.clone.dft_hbm, bf16[2,256,2048]{2,1,0:T(8,128)(2,1)} %constant.8.clone.tables, s32[1]{0:T(128)S(6)} %copy.9.block, s32[1]{0:T(128)S(6)} %copy.10.offset, ...), custom_call_target="tpu_custom_call" | custom-call | flops 8589934592 | bytes 20971520 | tf_op jit(solution)/shard_map/pallas_call | solution.py:473
  109.8 2.3 %copy.11 = bf16[16,256,128]{2,1,0:T(8,128)(2,1)} copy(bf16[16,256,128]{2,1,0:T(8,128)(2,1)} %shard_map.73) | data formatting | bytes 2097152

commit v5 on v4

--- a/solution.py
+++ b/solution.py
@@ -82,7 +82,9 @@
 SIDE = 4
 SLOTS = SIDE ** 3
 PIECE = 2 * 2 * BINS * W
-PARTS = ((0, 48, 48, (0, 1, 2)), (96, 48, 32, (1, 2, 0)), (176, 32, 48, (2, 0, 1)))
+PARTS = (((0, 96, (0, 1, 2)), (96, 80, (1, 2, 0)), (176, 80, (2, 0, 1))),
+         ((0, 80, (0, 1, 2)), (80, 96, (1, 2, 0)), (176, 80, (2, 0, 1))))
+LINES = (0, -1, 1, 2)
 ROUNDS = 2
 MESH = pl.DeviceIdType.MESH
 
@@ -312,42 +314,52 @@
 
     copies = {}
 
-    def start(turn, stage, part, kind):
-        first, low, high, order = PARTS[part]
-        first += turn * (PIECE // ROUNDS)
-        axis, full = order[stage], order[:stage]
-        if kind < 2 or stage < 2:
-            ref = slots(spectra, at, full, first, low + high)
-        else:
-            moved = list(at)
-            moved[axis] = lax.rem(at[axis] + (SIDE - 1 if kind == 2 else 1), SIDE)
-            ref = slots(spectra, moved, full, first + (0 if kind == 2 else low), low if kind == 2 else high)
-        index = ((turn * 3 + stage) * 3 + part) * 4 + kind
-        copy = pltpu.make_async_remote_copy(
+    def send(key, ref, axis, step):
+        index = len(copies)
+        copies[key] = pltpu.make_async_remote_copy(
             src_ref=ref, dst_ref=ref, send_sem=send_sem.at[index], recv_sem=recv_sem.at[index],
-            device_id=neighbour(axis, 2 if kind == 2 and stage < 2 else 1 if kind % 2 == 0 else -1),
-            device_id_type=MESH)
-        copies[turn, stage, part, kind] = copy
-        copy.start()
+            device_id=neighbour(axis, step), device_id_type=MESH)
+        copies[key].start()
+
+    def shifted(order, line, step):
+        moved = list(at)
+        for axis, by in ((order[1], LINES[line]), (order[2], step)):
+            moved[axis] = lax.rem(at[axis] + by + SIDE, SIDE)
+        return moved
 
     def begin(turn, stage):
-        for part in range(3):
-            start(turn, stage, part, 0)
-            start(turn, stage, part, 1)
-            if stage < 2:
-                start(turn, stage, part, 2)
-
-    def forward(turn, stage):
-        for part in range(3):
-            copies[turn, stage, part, 0].wait_recv()
-            start(turn, stage, part, 2)
-            copies[turn, stage, part, 1].wait_recv()
-            start(turn, stage, part, 3)
+        for part, (first, count, order) in enumerate(PARTS[turn]):
+            ref = slots(spectra, at, order[:stage], turn * 256 + first, count)
+            for kind, step in enumerate((1, -1, 2)):
+                send((turn, stage, part, kind), ref, order[stage], step)
 
     def finish(turn, stage):
         for part in range(3):
-            for kind in (2, 3) if stage == 2 else (0, 1, 2):
+            for kind in range(3):
                 copies[turn, stage, part, kind].wait_recv()
+
+    def send_line(turn, line):
+        for part, (first, count, order) in enumerate(PARTS[turn]):
+            if line:
+                copies[turn, 1, part, line - 1].wait_recv()
+            ref = slots(spectra, shifted(order, line, 0), order[:1], turn * 256 + first, count)
+            for kind, step in enumerate((1, -1)):
+                send((turn, 2, part, kind, line), ref, order[2], step)
+
+    def forward(turn, line):
+        for part, (first, count, order) in enumerate(PARTS[turn]):
+            low = (count // 32 + (count // 16) % 2 * (line % 2)) * 16
+            shares = ((1, -1, 0, low), (-1, 1, low, count - low))
+            for kind, (step, origin, skip, rows_sent) in enumerate(shares):
+                copies[turn, 2, part, kind, line].wait_recv()
+                ref = slots(spectra, shifted(order, line, origin), order[:1], turn * 256 + first + skip, rows_sent)
+                send((turn, 2, part, kind + 2, line), ref, order[2], step)
+
+    def finish_lines(turn):
+        for line in range(len(LINES)):
+            for part in range(3):
+                for kind in (2, 3):
+                    copies[turn, 2, part, kind, line].wait_recv()
 
     def multiply(turn):
         def step(index, _):
@@ -369,17 +381,11 @@
     group = 8
     width = group * SRC_BLOCK
 
-    def sum_lags(turn, core_index, store):
-        def step(n, _):
-            both = pl.ds(pl.multiple_of(core_index * columns + n * width, width), width)
-            value = jnp.dot(table[:, turn * 1024:(turn + 1) * 1024], cross[:, both],
-                            preferred_element_type=jnp.float32)
-            for i in range(group):
-                store(n * group + i, core_index * channels + n * group + i,
-                      value[:, i * SRC_BLOCK:(i + 1) * SRC_BLOCK])
-            return 0
-
-        lax.fori_loop(0, channels // group, step, 0)
+    def sum_lags(turn, core_index, n, store):
+        both = slice(core_index * columns + n * width, core_index * columns + (n + 1) * width)
+        value = jnp.dot(table[:, turn * 1024:(turn + 1) * 1024], cross[:, both], preferred_element_type=jnp.float32)
+        for i in range(group):
+            store(n * group + i, core_index * channels + n * group + i, value[:, i * SRC_BLOCK:(i + 1) * SRC_BLOCK])
 
     def keep(c, held_c, value):
         total[held_c] = value
@@ -400,31 +406,39 @@
     lax.fori_loop(24, 36, spread(1), 0)
     finish(0, 0)
     begin(0, 1)
+    send_line(0, 0)
     arrange(1)
     begin(1, 0)
-    lax.fori_loop(36, 56, spread(1), 0)
-    finish(0, 1)
-    begin(0, 2)
+    lax.fori_loop(36, 44, spread(1), 0)
+    for line in (1, 2, 3):
+        send_line(0, line)
     finish(1, 0)
     begin(1, 1)
-    lax.fori_loop(56, SLOTS, spread(1), 0)
-    forward(0, 2)
-    finish(1, 1)
-    begin(1, 2)
-    finish(0, 2)
+    forward(0, 0)
+    send_line(1, 0)
+    lax.fori_loop(44, SLOTS, spread(1), 0)
+    for line in (1, 2, 3):
+        forward(0, line)
+        send_line(1, line)
     own_table.wait()
-    lax.fori_loop(0, pairs, multiply(0), 0, unroll=2)
-    forward(1, 2)
-    sum_lags(0, 0, keep)
-    sum_lags(0, 1, keep)
-    finish(1, 2)
+    finish_lines(0)
+    quarter = pairs // 4
+    for line in range(4):
+        lax.fori_loop(line * quarter, (line + 1) * quarter, multiply(0), 0, unroll=2)
+        forward(1, line)
+    for core_index in range(2):
+        for n in range(channels // group):
+            sum_lags(0, core_index, n, keep)
+    finish_lines(1)
     lax.fori_loop(0, pairs, multiply(1), 0, unroll=2)
-    sum_lags(1, 1, hand_over)
+    for n in range(channels // group):
+        sum_lags(1, 1, n, hand_over)
     exchange = pltpu.make_async_remote_copy(
         src_ref=outgoing, dst_ref=incoming, send_sem=side_send.at[2], recv_sem=side_recv.at[2],
         device_id=sibling, device_id_type=MESH)
     exchange.start()
-    sum_lags(1, 0, conclude)
+    for n in range(channels // group):
+        sum_lags(1, 0, n, conclude)
     exchange.wait_recv()
 
     diagonal = (lax.broadcasted_iota(jnp.int32, (LAGS, LAGS), 0) == lax.broadcasted_iota(jnp.int32, (LAGS, LAGS), 1))
@@ -465,7 +479,7 @@
     lanes = channels * W
     columns = channels * SRC_BLOCK
     tiles = strain.reshape(channels // BINS, BINS, -1, R2).transpose(0, 2, 1, 3).reshape(-1, R2)
-    copies = ROUNDS * 3 * 3 * 4
+    copies = ROUNDS * 3 * (3 + 3 + 4 * len(LINES))
     anywhere = pl.BlockSpec(memory_space=pl.ANY)
     scalars = pl.BlockSpec(memory_space=pltpu.SMEM)
     dma = pltpu.SemaphoreType.DMA

time: 112 us -> 113 us (level)
  no operation moved by 1% of the time
where the time goes in v5:
time: 113 us; the launch traced here: 112 us
  Pallas kernels  109 us (96%)
  local copies, waits for them, and re-layouts  2.3 us (2%)
  between operations  1.31 us (1%)
    pallas_call x1, Pallas kernels, body(): pl.pallas_call(kernel, in_specs=[anywhere] * 4 + [scalars] * 3, out_specs...  109 us
    unnamed x1, local copies, waits for them, and re-layouts  2.3 us

profile of v5, /device:TPU:1, one launch (start us, length us, event | category | flops | bytes accessed | tf_op | source)
XLA Modules:
  0.0 112.4 jit_solution(8019610027367145889)
XLA Ops:
  1.3 108.8 %shard_map.73 = bf16[16,256,128]{2,1,0:T(8,128)(2,1)} custom-call(f32[4352,128]{1,0:T(8,128)} %bitcast.5, f32[96,128]{1,0:T(8,128)} %constant.6.clone.rows_hbm, bf16[128,256]{1,0:T(8,128)(2,1)} %constant.7.clone.dft_hbm, bf16[2,256,2048]{2,1,0:T(8,128)(2,1)} %constant.8.clone.tables, s32[1]{0:T(128)S(6)} %copy.9.block, s32[1]{0:T(128)S(6)} %copy.10.offset, ...), custom_call_target="tpu_custom_call" | custom-call | flops 8589934592 | bytes 20971520 | tf_op jit(solution)/shard_map/pallas_call | solution.py:487
  110.1 2.3 %copy.11 = bf16[16,256,128]{2,1,0:T(8,128)(2,1)} copy(bf16[16,256,128]{2,1,0:T(8,128)(2,1)} %shard_map.73) | data formatting | bytes 2097152

commit v6 on v5

--- a/solution.py
+++ b/solution.py
@@ -43,9 +43,9 @@
 
 
 def lag_table():
-    core, g, x, y_hi, y_lo, z_hi, z_lo, i = np.ix_(*[np.arange(n) for n in (2, 2, 4, 2, 2, 2, 2, 8)])
-    bins = 8 * x + 4 * y_hi + 2 * core + g + R1 * (32 * y_lo + 8 * (2 * z_hi + z_lo) + i)
-    lags = (np.arange(LAGS) - LAGS // 2).reshape((1, LAGS) + (1,) * 7)
+    core, g, x, y_hi, y_lo, z, i = np.ix_(*[np.arange(n) for n in (2, 2, 4, 2, 2, 4, 8)])
+    bins = 8 * x + 4 * y_hi + 2 * core + g + R1 * (32 * y_lo + 8 * z + i)
+    lags = (np.arange(LAGS) - LAGS // 2).reshape((1, LAGS) + (1,) * 6)
     angle = 2.0 * np.pi * (lags * bins[:, None] % L) / L
     table = np.stack([np.cos(angle), -np.sin(angle)], axis=7)
     return table.reshape(2, LAGS, NF).astype(np.float32)
@@ -122,9 +122,9 @@
     return along, across, [((x, y ^ 3, z), core), (at, 1 - core)]
 
 
-def kernel(strain_hbm, rows_hbm, dft_hbm, tables, block, offset, valid, out,
+def kernel(strain_hbm, rows_hbm, dft_hbm, tables, block, offset, valid, landed,
            strain, rows, dft, table, held, mixed, parts, share, bands, spectra, left, cross, total,
-           outgoing, incoming, turned, shipped, landed,
+           outgoing, incoming, turned, shipped,
            local_sem, send_sem, recv_sem, side_send, side_recv, chan_send, chan_recv, band_send, band_recv,
            ship_send, ship_recv):
     at, core = position()
@@ -361,22 +361,27 @@
                 for kind in (2, 3):
                     copies[turn, 2, part, kind, line].wait_recv()
 
-    def multiply(turn):
+    def multiply(turn, place=lambda index: index):
         def step(index, _):
-            results = []
-            for h in range(2):
-                k = index * 2 + h
-                s = spectra[k // 16, k // 8 % 2, k // 4 % 2, k % 4, turn * 256:(turn + 1) * 256, :]
-                right = jnp.concatenate([s, jnp.concatenate([-s[R2:], s[:R2]], axis=0)], axis=1)
-                results.append(jnp.dot(left[turn, k], right, preferred_element_type=jnp.float32))
-            base = pl.multiple_of(index * 32, 32)
+            k = place(index)
+            s = spectra[k // 16, k // 8 % 2, k // 4 % 2, k % 4, turn * 256:(turn + 1) * 256, :]
+            right = jnp.concatenate([s, jnp.concatenate([-s[R2:], s[:R2]], axis=0)], axis=1)
+            result = jnp.dot(left[turn, k], right, preferred_element_type=jnp.float32)
+            base = pl.multiple_of(k * 16, 16)
             for c in range(2 * channels):
-                both = jnp.concatenate([r[c * BINS:(c + 1) * BINS] for r in results], axis=0).astype(jnp.bfloat16)
-                cross[pl.ds(base, 16), c * SRC_BLOCK:(c + 1) * SRC_BLOCK] = both[:, :SRC_BLOCK]
-                cross[pl.ds(base + 16, 16), c * SRC_BLOCK:(c + 1) * SRC_BLOCK] = both[:, SRC_BLOCK:]
+                both = result[c * BINS:(c + 1) * BINS]
+                both = jnp.concatenate([both[:, :SRC_BLOCK], both[:, SRC_BLOCK:]], axis=0)
+                cross[pl.ds(base, 16), c * SRC_BLOCK:(c + 1) * SRC_BLOCK] = both.astype(jnp.bfloat16)
             return 0
 
         return step
+
+    def near(digit):
+        return digit + digit // 2
+
+    def shift(dx, dy, dz):
+        x, y, z = [lax.rem(a + b, SIDE) for a, b in zip(at, (dx, dy, dz))]
+        return x * 16 + y * 4 + z
 
     group = 8
     width = group * SRC_BLOCK
@@ -399,38 +404,44 @@
     pairs = SLOTS // 2
     lax.fori_loop(8, SLOTS, spread(0), 0)
     to_bands(0)
-    lax.fori_loop(0, 24, spread(1), 0)
+    lax.fori_loop(0, 8, spread(1), 0)
+    to_bands(1)
+    lax.fori_loop(8, 20, spread(1), 0)
     arrange(0)
     begin(0, 0)
-    to_bands(1)
-    lax.fori_loop(24, 36, spread(1), 0)
+    arrange(1)
+    begin(1, 0)
+    lax.fori_loop(20, 32, spread(1), 0)
     finish(0, 0)
     begin(0, 1)
     send_line(0, 0)
-    arrange(1)
-    begin(1, 0)
-    lax.fori_loop(36, 44, spread(1), 0)
+    finish(1, 0)
+    begin(1, 1)
+    send_line(1, 0)
+    lax.fori_loop(32, 44, spread(1), 0)
     for line in (1, 2, 3):
         send_line(0, line)
-    finish(1, 0)
-    begin(1, 1)
     forward(0, 0)
-    send_line(1, 0)
     lax.fori_loop(44, SLOTS, spread(1), 0)
     for line in (1, 2, 3):
         forward(0, line)
         send_line(1, line)
+    forward(1, 0)
     own_table.wait()
     finish_lines(0)
-    quarter = pairs // 4
-    for line in range(4):
-        lax.fori_loop(line * quarter, (line + 1) * quarter, multiply(0), 0, unroll=2)
+    quarter = SLOTS // 4
+    for line, turns in ((1, 1), (2, 1), (3, 2)):
+        first = (line - 1) * quarter
+        lax.fori_loop(first, first + turns * quarter, multiply(0), 0, unroll=4)
         forward(1, line)
     for core_index in range(2):
         for n in range(channels // group):
             sum_lags(0, core_index, n, keep)
+    lax.fori_loop(0, 27, multiply(1, lambda i: shift(near(i // 9), near(i // 3 % 3), near(i % 3))), 0, unroll=3)
     finish_lines(1)
-    lax.fori_loop(0, pairs, multiply(1), 0, unroll=2)
+    lax.fori_loop(0, 16, multiply(1, lambda i: shift(2, i // 4, i % 4)), 0, unroll=4)
+    lax.fori_loop(0, 12, multiply(1, lambda i: shift(near(i // 4), 2, i % 4)), 0, unroll=4)
+    lax.fori_loop(0, 9, multiply(1, lambda i: shift(near(i // 3), near(i % 3), 2)), 0, unroll=3)
     for n in range(channels // group):
         sum_lags(1, 1, n, hand_over)
     exchange = pltpu.make_async_remote_copy(
@@ -441,12 +452,11 @@
         sum_lags(1, 0, n, conclude)
     exchange.wait_recv()
 
-    diagonal = (lax.broadcasted_iota(jnp.int32, (LAGS, LAGS), 0) == lax.broadcasted_iota(jnp.int32, (LAGS, LAGS), 1))
-    unit = jnp.where(diagonal, 1.0, 0.0).astype(jnp.bfloat16)
+    unit = identity(SRC_BLOCK)
     last = (((1,), (1,)), ((), ()))
     for c in range(channels):
         value = (total[c] * FACTOR + incoming[c].astype(jnp.float32)).astype(jnp.bfloat16)
-        value = lax.dot_general(unit[:SRC_BLOCK, :SRC_BLOCK], value, last, preferred_element_type=jnp.float32)
+        value = lax.dot_general(unit, value, last, preferred_element_type=jnp.float32)
         for half in range(2):
             turned[half, pl.ds(c, SRC_BLOCK, stride=channels), :] = value[:, half * R2:(half + 1) * R2]
 
@@ -463,15 +473,30 @@
             device_id=device_at(place, which), device_id_type=MESH)
         ship.start()
         ships.append(ship)
-    landed[band] = pack(band)
+    shipped[band] = pack(band)
+    kept = pltpu.make_async_copy(shipped.at[band], landed.at[band], local_sem.at[0])
+    kept.start()
     for ship in ships:
         ship.wait_recv()
-    for s in range(SRC_BLOCK // (2 * SIDE)):
-        value = landed[:, s * channels:(s + 1) * channels, :].reshape(2 * SIDE * channels, LAGS)
-        out[s] = lax.dot_general(unit, value, last, preferred_element_type=jnp.float32).astype(out.dtype)
-
+
+    kept.wait()
     for copy in swaps + [exchange] + sums[0] + sums[1] + moves[0] + moves[1] + ships + list(copies.values()):
         copy.wait_send()
+
+
+def identity(n):
+    diagonal = lax.broadcasted_iota(jnp.int32, (n, n), 0) == lax.broadcasted_iota(jnp.int32, (n, n), 1)
+    return jnp.where(diagonal, 1.0, 0.0).astype(jnp.bfloat16)
+
+
+def turn_kernel(landed, out):
+    unit = identity(LAGS)
+    bands, rows, _ = landed.shape
+    channels = rows // out.shape[0]
+    for s in range(out.shape[0]):
+        value = landed[:, s * channels:(s + 1) * channels, :].reshape(bands * channels, LAGS)
+        value = lax.dot_general(unit, value, (((1,), (1,)), ((), ())), preferred_element_type=jnp.float32)
+        out[s] = value.astype(out.dtype)
 
 
 def body(strain, source_block, source_offset, window_valid):
@@ -484,11 +509,11 @@
     scalars = pl.BlockSpec(memory_space=pltpu.SMEM)
     dma = pltpu.SemaphoreType.DMA
     bf16, f32 = jnp.bfloat16, jnp.float32
-    return pl.pallas_call(
+    landed = pl.pallas_call(
         kernel,
         in_specs=[anywhere] * 4 + [scalars] * 3,
-        out_specs=pl.BlockSpec(memory_space=pltpu.VMEM),
-        out_shape=jax.ShapeDtypeStruct((SRC_BLOCK // (2 * SIDE), LAGS, 2 * SIDE * channels), bf16),
+        out_specs=anywhere,
+        out_shape=jax.ShapeDtypeStruct((2 * SIDE, 256, LAGS), bf16),
         scratch_shapes=[
             pltpu.VMEM(tiles.shape, f32),
             pltpu.VMEM((3 * R1, R2), f32),
@@ -507,7 +532,6 @@
             pltpu.VMEM((channels, LAGS, SRC_BLOCK), bf16),
             pltpu.VMEM((2, columns, R2), f32),
             pltpu.VMEM((2 * SIDE, 256, LAGS), bf16),
-            pltpu.VMEM((2 * SIDE, 256, LAGS), bf16),
             dma((4,)), dma((copies,)), dma((copies,)), dma((3,)), dma((3,)),
             dma((14,)), dma((14,)), dma((14,)), dma((14,)), dma((7,)), dma((7,)),
         ],
@@ -516,6 +540,14 @@
         cost_estimate=pl.CostEstimate(flops=4 * 256 * 4096 * 2048, bytes_accessed=20 * 2**20, transcendentals=0),
     )(tiles, jnp.asarray(row_tables()), jnp.asarray(short_dft(), dtype=bf16),
       jnp.asarray(lag_table(), dtype=bf16), source_block, source_offset, window_valid)
+    sources, steps = SRC_BLOCK // (2 * SIDE), 4
+    return pl.pallas_call(
+        turn_kernel,
+        grid=(steps,),
+        in_specs=[pl.BlockSpec((2 * SIDE, 256 // steps, LAGS), lambda i: (0, i, 0))],
+        out_specs=pl.BlockSpec((sources // steps, LAGS, 2 * SIDE * channels), lambda i: (i, 0, 0)),
+        out_shape=jax.ShapeDtypeStruct((sources, LAGS, 2 * SIDE * channels), bf16),
+    )(landed)
 
 
 def solution(mesh):

time: 113 us -> 111 us (0.982)
  local copies, waits for them, and re-layouts: 2.3 us -> 0 us
    pallas_call x0 -> x1, Pallas kernels: none -> 3.94 us  [body(): pl.pallas_call(turn_kernel, grid=(steps,), in_specs=[pl.BlockSpec((2 * SI...]
    pallas_call x1, Pallas kernels: 109 us -> 106 us  [body(): pl.pallas_call(kernel, in_specs=[anywhere] * 4 + [scalars] * 3, out_specs...]
    unnamed x1 -> x0, local copies, waits for them, and re-layouts: 2.3 us -> none
where the time goes in v6:
time: 111 us
  Pallas kernels  110 us (99%)
  between operations  1.31 us (1%)
    pallas_call x1, Pallas kernels, body(): pl.pallas_call(kernel, in_specs=[anywhere] * 4 + [scalars] * 3, out_specs...  106 us
    pallas_call x1, Pallas kernels, body(): pl.pallas_call(turn_kernel, grid=(steps,), in_specs=[pl.BlockSpec((2 * SI...  3.94 us

profile of v6, /device:TPU:1, one launch (start us, length us, event | category | flops | bytes accessed | tf_op | source)
XLA Modules:
  0.0 110.9 jit_solution(8528949452655114715)
XLA Ops:
  1.3 105.7 %shard_map.73.landed = bf16[8,256,256]{2,1,0:T(8,128)(2,1)} custom-call(f32[4352,128]{1,0:T(8,128)} %bitcast.5, f32[96,128]{1,0:T(8,128)} %constant.6.clone.rows_hbm, bf16[128,256]{1,0:T(8,128)(2,1)} %constant.7.clone.dft_hbm, bf16[2,256,2048]{2,1,0:T(8,128)(2,1)} %constant.8.clone.tables, s32[1]{0:T(128)S(6)} %copy.8.block, s32[1]{0:T(128)S(6)} %copy.9.offset, ...), custom_call_target="tpu_custom_call" | custom-call | flops 8589934592 | bytes 20971520 | tf_op jit(solution)/shard_map/pallas_call | solution.py:512
  107.0 3.9 %shard_map.74 = bf16[16,256,128]{2,1,0:T(8,128)(2,1)} custom-call(bf16[8,256,256]{2,1,0:T(8,128)(2,1)} %shard_map.73.landed), custom_call_target="tpu_custom_call" | custom-call | tf_op jit(solution)/shard_map/pallas_call | solution.py:544

commit v7 on v6

--- a/solution.py
+++ b/solution.py
@@ -417,22 +417,23 @@
     send_line(0, 0)
     finish(1, 0)
     begin(1, 1)
-    send_line(1, 0)
     lax.fori_loop(32, 44, spread(1), 0)
     for line in (1, 2, 3):
         send_line(0, line)
     forward(0, 0)
-    lax.fori_loop(44, SLOTS, spread(1), 0)
+    lax.fori_loop(44, 56, spread(1), 0)
+    forward(0, 1)
+    send_line(1, 0)
+    lax.fori_loop(56, SLOTS, spread(1), 0)
+    forward(0, 2)
+    forward(0, 3)
     for line in (1, 2, 3):
-        forward(0, line)
         send_line(1, line)
-    forward(1, 0)
     own_table.wait()
     finish_lines(0)
     quarter = SLOTS // 4
-    for line, turns in ((1, 1), (2, 1), (3, 2)):
-        first = (line - 1) * quarter
-        lax.fori_loop(first, first + turns * quarter, multiply(0), 0, unroll=4)
+    for line in range(4):
+        lax.fori_loop(line * quarter, (line + 1) * quarter, multiply(0), 0, unroll=4)
         forward(1, line)
     for core_index in range(2):
         for n in range(channels // group):

time: 111 us -> 108 us (0.973)
  Pallas kernels: 110 us -> 106 us
    pallas_call x1, Pallas kernels: 106 us -> 102 us  [body(): pl.pallas_call(kernel, in_specs=[anywhere] * 4 + [scalars] * 3, out_specs...]
where the time goes in v7:
time: 108 us; the launch traced here: 107 us
  Pallas kernels  106 us (98%)
  between operations  1.31 us (1%)
    pallas_call x1, Pallas kernels, body(): pl.pallas_call(kernel, in_specs=[anywhere] * 4 + [scalars] * 3, out_specs...  102 us
    pallas_call x1, Pallas kernels, body(): pl.pallas_call(turn_kernel, grid=(steps,), in_specs=[pl.BlockSpec((2 * SI...  3.94 us

profile of v7, /device:TPU:1, one launch (start us, length us, event | category | flops | bytes accessed | tf_op | source)
XLA Modules:
  0.0 107.4 jit_solution(10209592932900991850)
XLA Ops:
  1.3 102.2 %shard_map.73.landed = bf16[8,256,256]{2,1,0:T(8,128)(2,1)} custom-call(f32[4352,128]{1,0:T(8,128)} %bitcast.5, f32[96,128]{1,0:T(8,128)} %constant.6.clone.rows_hbm, bf16[128,256]{1,0:T(8,128)(2,1)} %constant.7.clone.dft_hbm, bf16[2,256,2048]{2,1,0:T(8,128)(2,1)} %constant.8.clone.tables, s32[1]{0:T(128)S(6)} %copy.8.block, s32[1]{0:T(128)S(6)} %copy.9.offset, ...), custom_call_target="tpu_custom_call" | custom-call | flops 8589934592 | bytes 20971520 | tf_op jit(solution)/shard_map/pallas_call | solution.py:513
  103.5 3.9 %shard_map.74 = bf16[16,256,128]{2,1,0:T(8,128)(2,1)} custom-call(bf16[8,256,256]{2,1,0:T(8,128)(2,1)} %shard_map.73.landed), custom_call_target="tpu_custom_call" | custom-call | tf_op jit(solution)/shard_map/pallas_call | solution.py:545

commit v8 on v7

--- a/solution.py
+++ b/solution.py
@@ -130,7 +130,7 @@
     at, core = position()
     chan, band = lax.axis_index("chan"), lax.axis_index("band")
     sibling = device_at(at, 1 - core)
-    lanes = held.shape[-1]
+    lanes = 2 * held.shape[-1]
     channels = lanes // W
     columns = channels * SRC_BLOCK
     along, across, rest = partners(at, core)
@@ -172,44 +172,110 @@
             folded[f, to, R2:] = gi.astype(jnp.bfloat16)
         return 0
 
-    lax.fori_loop(0, channels, fold, 0, unroll=2)
     dft_table = dft[...]
 
-    def transform(f, power):
-        y = lax.dot_general(dft_table, folded[f], (((1,), (1,)), ((), ())), preferred_element_type=jnp.float32)
-        total[f, :R2, :] = y[:, :R2]
-        total[f, R2:, :] = y[:, R2:]
-        square = (y * y).reshape(HALF // BINS, 2, BINS, lanes)
-        return power + (square[:, 0] + square[:, 1]).reshape(HALF, lanes)
-
-    power = lax.fori_loop(0, R1, transform, jnp.zeros((HALF, lanes), jnp.float32), unroll=8)
-    scales = []
-    for b in range(HALF // BINS):
-        mean = jnp.sum(power[b * BINS:(b + 1) * BINS], axis=0, keepdims=True) * (1.0 / 256.0)
-        scales.append(jnp.broadcast_to(lax.rsqrt(mean + 1e-06), (2 * BINS, lanes)))
-    scale = jnp.concatenate(scales, axis=0)
-
-    def finish_white(to, which, g):
+    def transform(half):
+        picked = slice(half * R2, (half + 1) * R2)
+
+        def step(f, power):
+            y = lax.dot_general(
+                dft_table, folded[f, picked, :], (((1,), (1,)), ((), ())), preferred_element_type=jnp.float32)
+            total[f, picked, :] = y
+            square = (y * y).reshape(HALF // BINS, 2, BINS, R2)
+            return power + (square[:, 0] + square[:, 1]).reshape(HALF, R2)
+
+        power = lax.fori_loop(0, R1, step, jnp.zeros((HALF, R2), jnp.float32), unroll=8)
+        scales = []
+        for b in range(HALF // BINS):
+            mean = jnp.sum(power[b * BINS:(b + 1) * BINS], axis=0, keepdims=True) * (1.0 / 256.0)
+            scales.append(jnp.broadcast_to(lax.rsqrt(mean + 1e-06), (2 * BINS, R2)))
+        return jnp.concatenate(scales, axis=0)
+
+    def finish_white(to, which, half, scale):
         def step(index, _):
-            f = index * 4 + which * 2 + g
-            y = jnp.concatenate([total[f, :R2, :], total[f, R2:, :]], axis=1)
-            held[to, g, index] = (y * scale).astype(jnp.bfloat16)
+            j, g = index // 2, index % 2
+            y = total[j * 4 + which * 2 + g, half * R2:(half + 1) * R2, :]
+            held[to, half, g, j] = (y * scale).astype(jnp.bfloat16)
             return 0
 
-        lax.fori_loop(0, SIDE * 2, step, 0, unroll=4)
-
-    for g in range(2):
-        finish_white(2, 1 - core, g)
+        lax.fori_loop(0, SIDE * 4, step, 0, unroll=4)
+
+    swaps, sums, moves = {}, {}, {}
+
+    def swap(half):
+        swaps[half] = pltpu.make_async_remote_copy(
+            src_ref=held.at[2, half], dst_ref=held.at[1, half], send_sem=side_send.at[half],
+            recv_sem=side_recv.at[half], device_id=sibling, device_id_type=MESH)
+        swaps[half].start()
+
+    chans = R1 // 2
+    spot = lax.broadcasted_iota(jnp.int32, (1, R2), 1)
+    stacked = jnp.zeros((1, R2), jnp.float32)
+    for w in range(W):
+        stacked = jnp.where(spot % W == w, jnp.where(valid[w] != 0, 1.0, 0.0), stacked)
+
+    def chosen(which, half):
+        source = band * channels + half * BINS + spot // W
+        first = jnp.where(which == block[0], 1, 0)
+        second = jnp.where(which == lax.rem(block[0] + 1, chans), 1, 0)
+        taken = jnp.where(source >= offset[0], first, second)
+        return jnp.where(taken == 1, stacked, 0.0)
+
+    slot = chan // 2
+
+    def add_up(half):
+        mine, theirs = chosen(chan, half), chosen(chan ^ 1, half)
+        swaps[half].wait_recv()
+
+        def mix(index, _):
+            j, g = index // 2, index % 2
+            value = held[0, half, g, j].astype(jnp.float32) * mine + held[1, half, g, j].astype(jnp.float32) * theirs
+            mixed[half, j, g] = value.astype(jnp.bfloat16)
+            return 0
+
+        lax.fori_loop(0, SIDE * 4, mix, 0, unroll=4)
+        sums[half] = []
+        for r, (place, which) in enumerate(along):
+            target = place[0] * 2 + place[1] // 2
+            sums[half].append(pltpu.make_async_remote_copy(
+                src_ref=mixed.at[half, target], dst_ref=parts.at[half, slot],
+                send_sem=chan_send.at[half * 7 + r], recv_sem=chan_recv.at[half * 7 + r],
+                device_id=device_at(place, which), device_id_type=MESH))
+        for copy in sums[half]:
+            copy.start()
+
+    def to_bands(half):
+        for copy in sums[half]:
+            copy.wait_recv()
+        parts[half, slot] = mixed[half, slot]
+        for g in range(2):
+            value = parts[half, 0, g].astype(jnp.float32)
+            for k in range(1, SIDE * 2):
+                value = value + parts[half, k, g].astype(jnp.float32)
+            share[half, :, g] = value.astype(jnp.bfloat16).reshape(2 * SIDE, 2 * BINS, R2)
+        moves[half] = []
+        for r, (place, which) in enumerate(across):
+            moves[half].append(pltpu.make_async_remote_copy(
+                src_ref=share.at[half, place[1] % 2 * SIDE + place[2]], dst_ref=bands.at[half, band],
+                send_sem=band_send.at[half * 7 + r], recv_sem=band_recv.at[half * 7 + r],
+                device_id=device_at(place, which), device_id_type=MESH))
+        for copy in moves[half]:
+            copy.start()
+        bands[half, band] = share[half, band]
+
+    lax.fori_loop(0, BINS, fold, 0, unroll=2)
+    scale = transform(0)
+    finish_white(2, 1 - core, 0, scale)
     pl.semaphore_wait(barrier, len(along) + len(across) + len(rest))
-    swaps = []
-    for g in range(2):
-        swap = pltpu.make_async_remote_copy(
-            src_ref=held.at[2, g], dst_ref=held.at[1, g], send_sem=side_send.at[g], recv_sem=side_recv.at[g],
-            device_id=sibling, device_id_type=MESH)
-        swap.start()
-        swaps.append(swap)
-    for g in range(2):
-        finish_white(0, core, g)
+    swap(0)
+    finish_white(0, core, 0, scale)
+    lax.fori_loop(BINS, BINS + 2, fold, 0, unroll=2)
+    add_up(0)
+    lax.fori_loop(BINS + 2, channels, fold, 0, unroll=2)
+    scale = transform(1)
+    finish_white(2, 1 - core, 1, scale)
+    swap(1)
+    finish_white(0, core, 1, scale)
 
     row = lax.broadcasted_iota(jnp.int32, (2 * BINS, R2), 0) % BINS
     lane = lax.broadcasted_iota(jnp.int32, (2 * BINS, R2), 1)
@@ -221,7 +287,7 @@
             picked = pl.ds(pl.multiple_of((y_lo * SIDE + z) * 16, 16), 16)
             for g in range(2):
                 for k in range(channels // 8):
-                    value = held[core_index, g, x * 2 + y_hi, picked, k * R2:(k + 1) * R2].astype(jnp.float32)
+                    value = held[core_index, k, g, x * 2 + y_hi, picked, :].astype(jnp.float32)
                     for ri in range(2):
                         even = pltpu.roll(value[ri * BINS:(ri + 1) * BINS], 0, 1, stride=W, stride_axis=0)
                         both = jnp.concatenate([even, pltpu.roll(even, R2 - W, 1)], axis=0)
@@ -236,66 +302,9 @@
 
     lax.fori_loop(0, 8, spread(0), 0)
 
-    spot = lax.broadcasted_iota(jnp.int32, (1, lanes), 1)
-    source = band * channels + spot // W
-    stacked = jnp.zeros((1, lanes), jnp.float32)
-    for w in range(W):
-        stacked = jnp.where(spot % W == w, jnp.where(valid[w] != 0, 1.0, 0.0), stacked)
-    chans = R1 // 2
-
-    def chosen(which):
-        first = jnp.where(which == block[0], 1, 0)
-        second = jnp.where(which == lax.rem(block[0] + 1, chans), 1, 0)
-        taken = jnp.where(source >= offset[0], first, second)
-        return jnp.where(taken == 1, stacked, 0.0)
-
-    mine, theirs = chosen(chan), chosen(chan ^ 1)
-    slot = chan // 2
-
-    def mix(g):
-        def step(index, _):
-            a, b = held[0, g, index], held[1, g, index]
-            value = a.astype(jnp.float32) * mine + b.astype(jnp.float32) * theirs
-            mixed[g, index] = value.astype(jnp.bfloat16)
-            return 0
-
-        return step
-
-    sums, moves = {}, {}
-    for g in range(2):
-        swaps[g].wait_recv()
-        lax.fori_loop(0, SIDE * 2, mix(g), 0, unroll=4)
-        sums[g] = []
-        for r, (place, which) in enumerate(along):
-            target = place[0] * 2 + place[1] // 2
-            sums[g].append(pltpu.make_async_remote_copy(
-                src_ref=mixed.at[g, target], dst_ref=parts.at[g, slot],
-                send_sem=chan_send.at[g * 7 + r], recv_sem=chan_recv.at[g * 7 + r],
-                device_id=device_at(place, which), device_id_type=MESH))
-        for copy in sums[g]:
-            copy.start()
-
-    def to_bands(g):
-        for copy in sums[g]:
-            copy.wait_recv()
-        parts[g, slot] = mixed[g, slot]
-        value = parts[g, 0].astype(jnp.float32)
-        for k in range(1, SIDE * 2):
-            value = value + parts[g, k].astype(jnp.float32)
-        share[g] = value.astype(jnp.bfloat16).reshape(2 * SIDE, 2 * BINS, lanes)
-        moves[g] = []
-        for r, (place, which) in enumerate(across):
-            moves[g].append(pltpu.make_async_remote_copy(
-                src_ref=share.at[g, place[1] % 2 * SIDE + place[2]], dst_ref=bands.at[g, band],
-                send_sem=band_send.at[g * 7 + r], recv_sem=band_recv.at[g * 7 + r],
-                device_id=device_at(place, which), device_id_type=MESH))
-        for copy in moves[g]:
-            copy.start()
-        bands[g, band] = share[g, band]
+    add_up(1)
 
     def arrange(g):
-        for copy in moves[g]:
-            copy.wait_recv()
         wide = (2 * BINS * W, lanes)
         same = lax.broadcasted_iota(jnp.int32, wide, 1) % W == lax.broadcasted_iota(jnp.int32, wide, 0) % W
         tall = (lanes, SRC_BLOCK)
@@ -305,7 +314,7 @@
         for b in range(2 * SIDE):
             goal = (channel + (b * channels + SRC_BLOCK) - offset[0]) % SRC_BLOCK
             pick = jnp.where(goal == column, 1.0, 0.0).astype(jnp.bfloat16)
-            part = bands[g, b].astype(jnp.float32)
+            part = jnp.concatenate([bands[half, b, g] for half in range(2)], axis=1).astype(jnp.float32)
             part = jnp.broadcast_to(part[:, None, :], (2 * BINS, W, lanes)).reshape(wide)
             part = jnp.where(same, part, 0.0).astype(jnp.bfloat16)
             term = jnp.dot(part, pick, preferred_element_type=jnp.float32)
@@ -402,16 +411,19 @@
         total[held_c] = total[held_c] + value
 
     pairs = SLOTS // 2
-    lax.fori_loop(8, SLOTS, spread(0), 0)
+    lax.fori_loop(8, 16, spread(0), 0)
     to_bands(0)
-    lax.fori_loop(0, 8, spread(1), 0)
+    lax.fori_loop(16, SLOTS, spread(0), 0)
     to_bands(1)
-    lax.fori_loop(8, 20, spread(1), 0)
+    lax.fori_loop(0, 24, spread(1), 0)
+    for half in range(2):
+        for copy in moves[half]:
+            copy.wait_recv()
     arrange(0)
     begin(0, 0)
     arrange(1)
     begin(1, 0)
-    lax.fori_loop(20, 32, spread(1), 0)
+    lax.fori_loop(24, 32, spread(1), 0)
     finish(0, 0)
     begin(0, 1)
     send_line(0, 0)
@@ -443,19 +455,23 @@
     lax.fori_loop(0, 16, multiply(1, lambda i: shift(2, i // 4, i % 4)), 0, unroll=4)
     lax.fori_loop(0, 12, multiply(1, lambda i: shift(near(i // 4), 2, i % 4)), 0, unroll=4)
     lax.fori_loop(0, 9, multiply(1, lambda i: shift(near(i // 3), near(i % 3), 2)), 0, unroll=3)
+    exchanges = []
     for n in range(channels // group):
         sum_lags(1, 1, n, hand_over)
-    exchange = pltpu.make_async_remote_copy(
-        src_ref=outgoing, dst_ref=incoming, send_sem=side_send.at[2], recv_sem=side_recv.at[2],
-        device_id=sibling, device_id_type=MESH)
-    exchange.start()
+        some = pl.ds(n * group, group)
+        exchange = pltpu.make_async_remote_copy(
+            src_ref=outgoing.at[some], dst_ref=incoming.at[some], send_sem=side_send.at[2 + n],
+            recv_sem=side_recv.at[2 + n], device_id=sibling, device_id_type=MESH)
+        exchange.start()
+        exchanges.append(exchange)
     for n in range(channels // group):
         sum_lags(1, 0, n, conclude)
-    exchange.wait_recv()
 
     unit = identity(SRC_BLOCK)
     last = (((1,), (1,)), ((), ()))
     for c in range(channels):
+        if c % group == 0:
+            exchanges[c // group].wait_recv()
         value = (total[c] * FACTOR + incoming[c].astype(jnp.float32)).astype(jnp.bfloat16)
         value = lax.dot_general(unit, value, last, preferred_element_type=jnp.float32)
         for half in range(2):
@@ -481,23 +497,13 @@
         ship.wait_recv()
 
     kept.wait()
-    for copy in swaps + [exchange] + sums[0] + sums[1] + moves[0] + moves[1] + ships + list(copies.values()):
+    for copy in [swaps[0], swaps[1]] + exchanges + sums[0] + sums[1] + moves[0] + moves[1] + ships + list(copies.values()):
         copy.wait_send()
 
 
 def identity(n):
     diagonal = lax.broadcasted_iota(jnp.int32, (n, n), 0) == lax.broadcasted_iota(jnp.int32, (n, n), 1)
     return jnp.where(diagonal, 1.0, 0.0).astype(jnp.bfloat16)
-
-
-def turn_kernel(landed, out):
-    unit = identity(LAGS)
-    bands, rows, _ = landed.shape
-    channels = rows // out.shape[0]
-    for s in range(out.shape[0]):
-        value = landed[:, s * channels:(s + 1) * channels, :].reshape(bands * channels, LAGS)
-        value = lax.dot_general(unit, value, (((1,), (1,)), ((), ())), preferred_element_type=jnp.float32)
-        out[s] = value.astype(out.dtype)
 
 
 def body(strain, source_block, source_offset, window_valid):
@@ -520,11 +526,11 @@
             pltpu.VMEM((3 * R1, R2), f32),
             pltpu.VMEM((R2, 2 * R2), bf16),
             pltpu.VMEM((LAGS, NF), bf16),
-            pltpu.VMEM((3, 2, SIDE * 2, R2, lanes), bf16),
-            pltpu.VMEM((2, SIDE * 2, R2, lanes), bf16),
-            pltpu.VMEM((2, SIDE * 2, R2, lanes), bf16),
-            pltpu.VMEM((2, SIDE * 2, 2 * BINS, lanes), bf16),
-            pltpu.VMEM((2, SIDE * 2, 2 * BINS, lanes), bf16),
+            pltpu.VMEM((3, 2, 2, SIDE * 2, R2, lanes // 2), bf16),
+            pltpu.VMEM((2, SIDE * 2, 2, R2, lanes // 2), bf16),
+            pltpu.VMEM((2, SIDE * 2, 2, R2, lanes // 2), bf16),
+            pltpu.VMEM((2, SIDE * 2, 2, 2 * BINS, lanes // 2), bf16),
+            pltpu.VMEM((2, SIDE * 2, 2, 2 * BINS, lanes // 2), bf16),
             pltpu.VMEM((SIDE, 2, 2, SIDE, PIECE, SRC_BLOCK), bf16),
             pltpu.VMEM((2, SLOTS, 256, 256), bf16),
             pltpu.VMEM((NF // 2, 2 * columns), bf16),
@@ -533,7 +539,7 @@
             pltpu.VMEM((channels, LAGS, SRC_BLOCK), bf16),
             pltpu.VMEM((2, columns, R2), f32),
             pltpu.VMEM((2 * SIDE, 256, LAGS), bf16),
-            dma((4,)), dma((copies,)), dma((copies,)), dma((3,)), dma((3,)),
+            dma((4,)), dma((copies,)), dma((copies,)), dma((4,)), dma((4,)),
             dma((14,)), dma((14,)), dma((14,)), dma((14,)), dma((7,)), dma((7,)),
         ],
         compiler_params=pltpu.CompilerParams(
@@ -541,14 +547,9 @@
         cost_estimate=pl.CostEstimate(flops=4 * 256 * 4096 * 2048, bytes_accessed=20 * 2**20, transcendentals=0),
     )(tiles, jnp.asarray(row_tables()), jnp.asarray(short_dft(), dtype=bf16),
       jnp.asarray(lag_table(), dtype=bf16), source_block, source_offset, window_valid)
-    sources, steps = SRC_BLOCK // (2 * SIDE), 4
-    return pl.pallas_call(
-        turn_kernel,
-        grid=(steps,),
-        in_specs=[pl.BlockSpec((2 * SIDE, 256 // steps, LAGS), lambda i: (0, i, 0))],
-        out_specs=pl.BlockSpec((sources // steps, LAGS, 2 * SIDE * channels), lambda i: (i, 0, 0)),
-        out_shape=jax.ShapeDtypeStruct((sources, LAGS, 2 * SIDE * channels), bf16),
-    )(landed)
+    rows = landed.reshape(2 * SIDE, -1, channels, LAGS)
+    turned = jnp.einsum("tu,bscu->stbc", jnp.eye(LAGS, dtype=bf16), rows, preferred_element_type=f32)
+    return turned.astype(bf16).reshape(-1, LAGS, 2 * SIDE * channels)
 
 
 def solution(mesh):

time: 108 us -> 111 us (1.028)
  matrix products: 0 us -> 1.69 us
  local copies, waits for them, and re-layouts: 0 us -> 1.42 us
    pallas_call x1, Pallas kernels: 102 us -> 106 us  [body(): pl.pallas_call(kernel, in_specs=[anywhere] * 4 + [scalars] * 3, out_specs...]
    pallas_call x1 -> x0, Pallas kernels: 3.94 us -> none  [body(): pl.pallas_call(turn_kernel, grid=(steps,), in_specs=[pl.BlockSpec((2 * SI...]
    dot_general x0 -> x1, matrix products: none -> 1.69 us  [body(): jnp.einsum('tu,bscu->stbc', jnp.eye(LAGS, dtype=bf16), rows, preferred_el...]
    reshape x0 -> x1, local copies, waits for them, and re-layouts: none -> 1.31 us  [body(): return turned.astype(bf16).reshape(-1, LAGS, 2 * SIDE * channels)]
where the time goes in v8:
time: 111 us
  Pallas kernels  106 us (95%)
  matrix products  1.69 us (2%)
  local copies, waits for them, and re-layouts  1.42 us (1%)
  between operations  1.32 us (1%)
    pallas_call x1, Pallas kernels, body(): pl.pallas_call(kernel, in_specs=[anywhere] * 4 + [scalars] * 3, out_specs...  106 us

profile of v8, /device:TPU:1, one launch (start us, length us, event | category | flops | bytes accessed | tf_op | source)
XLA Modules:
  0.0 110.8 jit_solution(17151061539846555251)
XLA Ops:
  1.3 106.4 %shard_map.73 = bf16[8,256,256]{2,1,0:T(8,128)(2,1)} custom-call(f32[4352,128]{1,0:T(8,128)} %bitcast.17, f32[96,128]{1,0:T(8,128)} %constant.6.clone.rows_hbm, bf16[128,256]{1,0:T(8,128)(2,1)} %constant.7.clone.dft_hbm, bf16[2,256,2048]{2,1,0:T(8,128)(2,1)} %constant.8.clone.tables, s32[1]{0:T(128)S(6)} %copy.11.block, s32[1]{0:T(128)S(6)} %copy.12.offset, ...), custom_call_target="tpu_custom_call" | custom-call | flops 8589934592 | bytes 20971520 | tf_op jit(solution)/shard_map/pallas_call | solution.py:519
  107.7 1.7 %fusion = bf16[16,256,8,16]{1,3,0,2:T(8,128)(2,1)S(1)} fusion(bf16[8,16,16,256]{3,2,1,0:T(8,128)(2,1)} %bitcast.16), kind=kOutput, calls=%fused_computation.1 | convolution fusion | flops 269025280 | bytes 2097152 | tf_op jit(solution)/shard_map/tu,bscu->stbc/dot_general | solution.py:551
  109.4 0.1 copy.8
  109.5 1.3 %copy.9 = bf16[16,256,128]{2,1,0:T(8,128)(2,1)} copy(bf16[16,256,128]{1,2,0:T(8,128)(2,1)S(1)} %bitcast.15) | data formatting | bytes 2097152 | tf_op jit(solution)/shard_map/reshape | solution.py:552

commit v9 on v7

--- a/solution.py
+++ b/solution.py
@@ -406,22 +406,22 @@
     to_bands(0)
     lax.fori_loop(0, 8, spread(1), 0)
     to_bands(1)
-    lax.fori_loop(8, 20, spread(1), 0)
+    lax.fori_loop(8, 28, spread(1), 0)
     arrange(0)
     begin(0, 0)
     arrange(1)
     begin(1, 0)
-    lax.fori_loop(20, 32, spread(1), 0)
+    lax.fori_loop(28, 36, spread(1), 0)
     finish(0, 0)
     begin(0, 1)
     send_line(0, 0)
     finish(1, 0)
     begin(1, 1)
-    lax.fori_loop(32, 44, spread(1), 0)
+    lax.fori_loop(36, 46, spread(1), 0)
     for line in (1, 2, 3):
         send_line(0, line)
     forward(0, 0)
-    lax.fori_loop(44, 56, spread(1), 0)
+    lax.fori_loop(46, 56, spread(1), 0)
     forward(0, 1)
     send_line(1, 0)
     lax.fori_loop(56, SLOTS, spread(1), 0)
@@ -443,19 +443,23 @@
     lax.fori_loop(0, 16, multiply(1, lambda i: shift(2, i // 4, i % 4)), 0, unroll=4)
     lax.fori_loop(0, 12, multiply(1, lambda i: shift(near(i // 4), 2, i % 4)), 0, unroll=4)
     lax.fori_loop(0, 9, multiply(1, lambda i: shift(near(i // 3), near(i % 3), 2)), 0, unroll=3)
+    exchanges = []
     for n in range(channels // group):
         sum_lags(1, 1, n, hand_over)
-    exchange = pltpu.make_async_remote_copy(
-        src_ref=outgoing, dst_ref=incoming, send_sem=side_send.at[2], recv_sem=side_recv.at[2],
-        device_id=sibling, device_id_type=MESH)
-    exchange.start()
+        some = pl.ds(n * group, group)
+        exchange = pltpu.make_async_remote_copy(
+            src_ref=outgoing.at[some], dst_ref=incoming.at[some], send_sem=side_send.at[2 + n],
+            recv_sem=side_recv.at[2 + n], device_id=sibling, device_id_type=MESH)
+        exchange.start()
+        exchanges.append(exchange)
     for n in range(channels // group):
         sum_lags(1, 0, n, conclude)
-    exchange.wait_recv()
 
     unit = identity(SRC_BLOCK)
     last = (((1,), (1,)), ((), ()))
     for c in range(channels):
+        if c % group == 0:
+            exchanges[c // group].wait_recv()
         value = (total[c] * FACTOR + incoming[c].astype(jnp.float32)).astype(jnp.bfloat16)
         value = lax.dot_general(unit, value, last, preferred_element_type=jnp.float32)
         for half in range(2):
@@ -463,41 +467,32 @@
 
     def pack(index):
         picked = pl.ds(pl.multiple_of(index * 256, 256), 256)
-        return jnp.concatenate([turned[0, picked, :], turned[1, picked, :]], axis=1).astype(jnp.bfloat16)
+        both = jnp.concatenate([turned[0, picked, :], turned[1, picked, :]], axis=1).astype(jnp.bfloat16)
+        return both.reshape(-1, channels, LAGS)
 
     ships = []
     for r, (place, which) in enumerate(across):
         index = place[1] % 2 * SIDE + place[2]
         shipped[index] = pack(index)
         ship = pltpu.make_async_remote_copy(
-            src_ref=shipped.at[index], dst_ref=landed.at[band], send_sem=ship_send.at[r], recv_sem=ship_recv.at[r],
+            src_ref=shipped.at[index], dst_ref=landed.at[:, band], send_sem=ship_send.at[r], recv_sem=ship_recv.at[r],
             device_id=device_at(place, which), device_id_type=MESH)
         ship.start()
         ships.append(ship)
     shipped[band] = pack(band)
-    kept = pltpu.make_async_copy(shipped.at[band], landed.at[band], local_sem.at[0])
+    kept = pltpu.make_async_copy(shipped.at[band], landed.at[:, band], local_sem.at[0])
     kept.start()
     for ship in ships:
         ship.wait_recv()
 
     kept.wait()
-    for copy in swaps + [exchange] + sums[0] + sums[1] + moves[0] + moves[1] + ships + list(copies.values()):
+    for copy in swaps + exchanges + sums[0] + sums[1] + moves[0] + moves[1] + ships + list(copies.values()):
         copy.wait_send()
 
 
 def identity(n):
     diagonal = lax.broadcasted_iota(jnp.int32, (n, n), 0) == lax.broadcasted_iota(jnp.int32, (n, n), 1)
     return jnp.where(diagonal, 1.0, 0.0).astype(jnp.bfloat16)
-
-
-def turn_kernel(landed, out):
-    unit = identity(LAGS)
-    bands, rows, _ = landed.shape
-    channels = rows // out.shape[0]
-    for s in range(out.shape[0]):
-        value = landed[:, s * channels:(s + 1) * channels, :].reshape(bands * channels, LAGS)
-        value = lax.dot_general(unit, value, (((1,), (1,)), ((), ())), preferred_element_type=jnp.float32)
-        out[s] = value.astype(out.dtype)
 
 
 def body(strain, source_block, source_offset, window_valid):
@@ -514,7 +509,7 @@
         kernel,
         in_specs=[anywhere] * 4 + [scalars] * 3,
         out_specs=anywhere,
-        out_shape=jax.ShapeDtypeStruct((2 * SIDE, 256, LAGS), bf16),
+        out_shape=jax.ShapeDtypeStruct((SRC_BLOCK // (2 * SIDE), 2 * SIDE, channels, LAGS), bf16),
         scratch_shapes=[
             pltpu.VMEM(tiles.shape, f32),
             pltpu.VMEM((3 * R1, R2), f32),
@@ -532,8 +527,8 @@
             pltpu.VMEM((channels, LAGS, SRC_BLOCK), bf16),
             pltpu.VMEM((channels, LAGS, SRC_BLOCK), bf16),
             pltpu.VMEM((2, columns, R2), f32),
-            pltpu.VMEM((2 * SIDE, 256, LAGS), bf16),
-            dma((4,)), dma((copies,)), dma((copies,)), dma((3,)), dma((3,)),
+            pltpu.VMEM((2 * SIDE, SRC_BLOCK // (2 * SIDE), channels, LAGS), bf16),
+            dma((4,)), dma((copies,)), dma((copies,)), dma((4,)), dma((4,)),
             dma((14,)), dma((14,)), dma((14,)), dma((14,)), dma((7,)), dma((7,)),
         ],
         compiler_params=pltpu.CompilerParams(
@@ -541,14 +536,8 @@
         cost_estimate=pl.CostEstimate(flops=4 * 256 * 4096 * 2048, bytes_accessed=20 * 2**20, transcendentals=0),
     )(tiles, jnp.asarray(row_tables()), jnp.asarray(short_dft(), dtype=bf16),
       jnp.asarray(lag_table(), dtype=bf16), source_block, source_offset, window_valid)
-    sources, steps = SRC_BLOCK // (2 * SIDE), 4
-    return pl.pallas_call(
-        turn_kernel,
-        grid=(steps,),
-        in_specs=[pl.BlockSpec((2 * SIDE, 256 // steps, LAGS), lambda i: (0, i, 0))],
-        out_specs=pl.BlockSpec((sources // steps, LAGS, 2 * SIDE * channels), lambda i: (i, 0, 0)),
-        out_shape=jax.ShapeDtypeStruct((sources, LAGS, 2 * SIDE * channels), bf16),
-    )(landed)
+    rows = landed.reshape(-1, 2 * SIDE * channels, LAGS)
+    return jnp.einsum("tu,scu->stc", jnp.eye(LAGS, dtype=bf16), rows, preferred_element_type=f32).astype(bf16)
 
 
 def solution(mesh):

time: 108 us -> 108 us (level)
  Pallas kernels: 106 us -> 104 us
  matrix products: 0 us -> 1.69 us
  local copies, waits for them, and re-layouts: 0 us -> 1.31 us
    pallas_call x1 -> x0, Pallas kernels: 3.94 us -> none  [body(): pl.pallas_call(turn_kernel, grid=(steps,), in_specs=[pl.BlockSpec((2 * SI...]
    dot_general x0 -> x1, matrix products: none -> 1.69 us  [body(): jnp.einsum('tu,scu->stc', jnp.eye(LAGS, dtype=bf16), rows, preferred_elem...]
    pallas_call x1, Pallas kernels: 102 us -> 104 us  [body(): pl.pallas_call(kernel, in_specs=[anywhere] * 4 + [scalars] * 3, out_specs...]
    convert_element_type x0 -> x1, local copies, waits for them, and re-layouts: none -> 1.31 us  [body(): jnp.einsum('tu,scu->stc', jnp.eye(LAGS, dtype=bf16), rows, preferred_elem...]
where the time goes in v9:
time: 108 us
  Pallas kernels  104 us (96%)
  matrix products  1.69 us (2%)
  local copies, waits for them, and re-layouts  1.31 us (1%)
  between operations  1.31 us (1%)
    pallas_call x1, Pallas kernels, body(): pl.pallas_call(kernel, in_specs=[anywhere] * 4 + [scalars] * 3, out_specs...  104 us

profile of v9, /device:TPU:1, one launch (start us, length us, event | category | flops | bytes accessed | tf_op | source)
XLA Modules:
  0.0 108.0 jit_solution(13603265480266885854)
XLA Ops:
  1.3 103.7 %shard_map.73 = bf16[16,8,16,256]{3,2,1,0:T(8,128)(2,1)} custom-call(f32[4352,128]{1,0:T(8,128)} %bitcast.13, f32[96,128]{1,0:T(8,128)} %constant.6.clone.rows_hbm, bf16[128,256]{1,0:T(8,128)(2,1)} %constant.7.clone.dft_hbm, bf16[2,256,2048]{2,1,0:T(8,128)(2,1)} %constant.8.clone.tables, s32[1]{0:T(128)S(6)} %copy.9.block, s32[1]{0:T(128)S(6)} %copy.10.offset, ...), custom_call_target="tpu_custom_call" | custom-call | flops 8589934592 | bytes 20971520 | tf_op jit(solution)/shard_map/pallas_call | solution.py:508
  105.0 1.7 %fusion = bf16[16,256,128]{1,2,0:T(8,128)(2,1)S(1)} fusion(bf16[16,128,256]{2,1,0:T(8,128)(2,1)} %bitcast.12), kind=kOutput, calls=%fused_computation.1 | convolution fusion | flops 269025280 | bytes 2097152 | tf_op jit(solution)/shard_map/tu,scu->stc/dot_general | solution.py:540
  106.7 1.3 %copy.8 = bf16[16,256,128]{2,1,0:T(8,128)(2,1)} copy(bf16[16,256,128]{1,2,0:T(8,128)(2,1)S(1)} %fusion) | data formatting | bytes 2097152 | tf_op jit(solution)/shard_map/convert_element_type | solution.py:540

commit v10 on v9

--- a/solution.py
+++ b/solution.py
@@ -224,17 +224,17 @@
                     value = held[core_index, g, x * 2 + y_hi, picked, k * R2:(k + 1) * R2].astype(jnp.float32)
                     for ri in range(2):
                         even = pltpu.roll(value[ri * BINS:(ri + 1) * BINS], 0, 1, stride=W, stride_axis=0)
-                        both = jnp.concatenate([even, pltpu.roll(even, R2 - W, 1)], axis=0)
+                        both = jnp.concatenate([even, pltpu.roll(even, R2 - W, 1)], axis=0).astype(jnp.bfloat16)
                         for t in range(4):
                             moved = pltpu.roll(both, R2 - 2 * W * t, 1) if t else both
                             first = ((core_index * channels // 8 + k) * 4 + t) * 2 * BINS
                             left[g, index, first:first + 2 * BINS, ri * R2:(ri + 1) * R2] = jnp.where(
-                                own, moved, 0.0).astype(jnp.bfloat16)
+                                own, moved, jnp.zeros_like(moved))
             return 0
 
         return step
 
-    lax.fori_loop(0, 8, spread(0), 0)
+    lax.fori_loop(0, 8, spread(0), 0, unroll=4)
 
     spot = lax.broadcasted_iota(jnp.int32, (1, lanes), 1)
     source = band * channels + spot // W
@@ -402,29 +402,29 @@
         total[held_c] = total[held_c] + value
 
     pairs = SLOTS // 2
-    lax.fori_loop(8, SLOTS, spread(0), 0)
+    lax.fori_loop(8, SLOTS, spread(0), 0, unroll=4)
     to_bands(0)
-    lax.fori_loop(0, 8, spread(1), 0)
+    lax.fori_loop(0, 16, spread(1), 0, unroll=4)
     to_bands(1)
-    lax.fori_loop(8, 28, spread(1), 0)
+    lax.fori_loop(16, 32, spread(1), 0, unroll=4)
     arrange(0)
     begin(0, 0)
     arrange(1)
     begin(1, 0)
-    lax.fori_loop(28, 36, spread(1), 0)
+    lax.fori_loop(32, 40, spread(1), 0, unroll=4)
     finish(0, 0)
     begin(0, 1)
     send_line(0, 0)
     finish(1, 0)
     begin(1, 1)
-    lax.fori_loop(36, 46, spread(1), 0)
+    lax.fori_loop(40, 48, spread(1), 0, unroll=4)
     for line in (1, 2, 3):
         send_line(0, line)
     forward(0, 0)
-    lax.fori_loop(46, 56, spread(1), 0)
+    lax.fori_loop(48, 56, spread(1), 0, unroll=4)
     forward(0, 1)
     send_line(1, 0)
-    lax.fori_loop(56, SLOTS, spread(1), 0)
+    lax.fori_loop(56, SLOTS, spread(1), 0, unroll=4)
     forward(0, 2)
     forward(0, 3)
     for line in (1, 2, 3):

time: 108 us -> 103 us (0.954)
  Pallas kernels: 104 us -> 98.4 us
    pallas_call x1, Pallas kernels: 104 us -> 98.4 us  [body(): pl.pallas_call(kernel, in_specs=[anywhere] * 4 + [scalars] * 3, out_specs...]
where the time goes in v10:
time: 103 us
  Pallas kernels  98.4 us (96%)
  matrix products  1.7 us (2%)
  local copies, waits for them, and re-layouts  1.31 us (1%)
  between operations  1.31 us (1%)
    pallas_call x1, Pallas kernels, body(): pl.pallas_call(kernel, in_specs=[anywhere] * 4 + [scalars] * 3, out_specs...  98.4 us

profile of v10, /device:TPU:1, one launch (start us, length us, event | category | flops | bytes accessed | tf_op | source)
XLA Modules:
  0.0 102.7 jit_solution(17106243145116021924)
XLA Ops:
  1.3 98.4 %shard_map.73 = bf16[16,8,16,256]{3,2,1,0:T(8,128)(2,1)} custom-call(f32[4352,128]{1,0:T(8,128)} %bitcast.13, f32[96,128]{1,0:T(8,128)} %constant.6.clone.rows_hbm, bf16[128,256]{1,0:T(8,128)(2,1)} %constant.7.clone.dft_hbm, bf16[2,256,2048]{2,1,0:T(8,128)(2,1)} %constant.8.clone.tables, s32[1]{0:T(128)S(6)} %copy.9.block, s32[1]{0:T(128)S(6)} %copy.10.offset, ...), custom_call_target="tpu_custom_call" | custom-call | flops 8589934592 | bytes 20971520 | tf_op jit(solution)/shard_map/pallas_call | solution.py:508
  99.7 1.7 %fusion = bf16[16,256,128]{1,2,0:T(8,128)(2,1)S(1)} fusion(bf16[16,128,256]{2,1,0:T(8,128)(2,1)} %bitcast.12), kind=kOutput, calls=%fused_computation.1 | convolution fusion | flops 269025280 | bytes 2097152 | tf_op jit(solution)/shard_map/tu,scu->stc/dot_general | solution.py:540
  101.4 1.3 %copy.8 = bf16[16,256,128]{2,1,0:T(8,128)(2,1)} copy(bf16[16,256,128]{1,2,0:T(8,128)(2,1)S(1)} %fusion) | data formatting | bytes 2097152 | tf_op jit(solution)/shard_map/convert_element_type | solution.py:540

commit v11 on v10

--- a/solution.py
+++ b/solution.py
@@ -124,7 +124,7 @@
 
 def kernel(strain_hbm, rows_hbm, dft_hbm, tables, block, offset, valid, landed,
            strain, rows, dft, table, held, mixed, parts, share, bands, spectra, left, cross, total,
-           outgoing, incoming, turned, shipped,
+           outgoing, incoming, turned, shipped, picks,
            local_sem, send_sem, recv_sem, side_send, side_recv, chan_send, chan_recv, band_send, band_recv,
            ship_send, ship_recv):
     at, core = position()
@@ -293,23 +293,23 @@
             copy.start()
         bands[g, band] = share[g, band]
 
+    def select():
+        tall = (2 * SIDE * lanes, SRC_BLOCK)
+        source = lax.broadcasted_iota(jnp.int32, tall, 0) // W
+        goal = (source + SRC_BLOCK - offset[0]) % SRC_BLOCK
+        picks[...] = jnp.where(goal == lax.broadcasted_iota(jnp.int32, tall, 1), 1.0, 0.0).astype(jnp.bfloat16)
+
     def arrange(g):
         for copy in moves[g]:
             copy.wait_recv()
         wide = (2 * BINS * W, lanes)
         same = lax.broadcasted_iota(jnp.int32, wide, 1) % W == lax.broadcasted_iota(jnp.int32, wide, 0) % W
-        tall = (lanes, SRC_BLOCK)
-        channel = lax.broadcasted_iota(jnp.int32, tall, 0) // W
-        column = lax.broadcasted_iota(jnp.int32, tall, 1)
-        value = None
+        spaced = []
         for b in range(2 * SIDE):
-            goal = (channel + (b * channels + SRC_BLOCK) - offset[0]) % SRC_BLOCK
-            pick = jnp.where(goal == column, 1.0, 0.0).astype(jnp.bfloat16)
             part = bands[g, b].astype(jnp.float32)
             part = jnp.broadcast_to(part[:, None, :], (2 * BINS, W, lanes)).reshape(wide)
-            part = jnp.where(same, part, 0.0).astype(jnp.bfloat16)
-            term = jnp.dot(part, pick, preferred_element_type=jnp.float32)
-            value = term if value is None else value + term
+            spaced.append(jnp.where(same, part, 0.0).astype(jnp.bfloat16))
+        value = jnp.dot(jnp.concatenate(spaced, axis=1), picks[...], preferred_element_type=jnp.float32)
         spectra[at[0], at[1] // 2, at[1] % 2, at[2], g * wide[0]:(g + 1) * wide[0], :] = value.astype(jnp.bfloat16)
 
     copies = {}
@@ -403,28 +403,27 @@
 
     pairs = SLOTS // 2
     lax.fori_loop(8, SLOTS, spread(0), 0, unroll=4)
+    select()
+    lax.fori_loop(0, 40, spread(1), 0, unroll=4)
     to_bands(0)
-    lax.fori_loop(0, 16, spread(1), 0, unroll=4)
+    lax.fori_loop(40, 52, spread(1), 0, unroll=4)
     to_bands(1)
-    lax.fori_loop(16, 32, spread(1), 0, unroll=4)
+    lax.fori_loop(52, 60, spread(1), 0, unroll=4)
     arrange(0)
     begin(0, 0)
     arrange(1)
     begin(1, 0)
-    lax.fori_loop(32, 40, spread(1), 0, unroll=4)
+    lax.fori_loop(60, SLOTS, spread(1), 0, unroll=4)
     finish(0, 0)
     begin(0, 1)
     send_line(0, 0)
     finish(1, 0)
     begin(1, 1)
-    lax.fori_loop(40, 48, spread(1), 0, unroll=4)
     for line in (1, 2, 3):
         send_line(0, line)
     forward(0, 0)
-    lax.fori_loop(48, 56, spread(1), 0, unroll=4)
     forward(0, 1)
     send_line(1, 0)
-    lax.fori_loop(56, SLOTS, spread(1), 0, unroll=4)
     forward(0, 2)
     forward(0, 3)
     for line in (1, 2, 3):
@@ -528,6 +527,7 @@
             pltpu.VMEM((channels, LAGS, SRC_BLOCK), bf16),
             pltpu.VMEM((2, columns, R2), f32),
             pltpu.VMEM((2 * SIDE, SRC_BLOCK // (2 * SIDE), channels, LAGS), bf16),
+            pltpu.VMEM((2 * SIDE * lanes, SRC_BLOCK), bf16),
             dma((4,)), dma((copies,)), dma((copies,)), dma((4,)), dma((4,)),
             dma((14,)), dma((14,)), dma((14,)), dma((14,)), dma((7,)), dma((7,)),
         ],

time: 103 us -> 102 us (level)
  no operation moved by 1% of the time
where the time goes in v11:
time: 102 us
  Pallas kernels  97.8 us (96%)
  matrix products  1.69 us (2%)
  local copies, waits for them, and re-layouts  1.31 us (1%)
  between operations  1.31 us (1%)
    pallas_call x1, Pallas kernels, body(): pl.pallas_call(kernel, in_specs=[anywhere] * 4 + [scalars] * 3, out_specs...  97.8 us

profile of v11, /device:TPU:1, one launch (start us, length us, event | category | flops | bytes accessed | tf_op | source)
XLA Modules:
  0.0 102.1 jit_solution(6193281868732044667)
XLA Ops:
  1.3 97.8 %shard_map.73 = bf16[16,8,16,256]{3,2,1,0:T(8,128)(2,1)} custom-call(f32[4352,128]{1,0:T(8,128)} %bitcast.13, f32[96,128]{1,0:T(8,128)} %constant.6.clone.rows_hbm, bf16[128,256]{1,0:T(8,128)(2,1)} %constant.7.clone.dft_hbm, bf16[2,256,2048]{2,1,0:T(8,128)(2,1)} %constant.8.clone.tables, s32[1]{0:T(128)S(6)} %copy.9.block, s32[1]{0:T(128)S(6)} %copy.10.offset, ...), custom_call_target="tpu_custom_call" | custom-call | flops 8589934592 | bytes 20971520 | tf_op jit(solution)/shard_map/pallas_call | solution.py:507
  99.1 1.7 %fusion = bf16[16,256,128]{1,2,0:T(8,128)(2,1)S(1)} fusion(bf16[16,128,256]{2,1,0:T(8,128)(2,1)} %bitcast.12), kind=kOutput, calls=%fused_computation.1 | convolution fusion | flops 269025280 | bytes 2097152 | tf_op jit(solution)/shard_map/tu,scu->stc/dot_general | solution.py:540
  100.8 1.3 %copy.8 = bf16[16,256,128]{2,1,0:T(8,128)(2,1)} copy(bf16[16,256,128]{1,2,0:T(8,128)(2,1)S(1)} %fusion) | data formatting | bytes 2097152 | tf_op jit(solution)/shard_map/convert_element_type | solution.py:540

commit v12 on v11

--- a/solution.py
+++ b/solution.py
@@ -429,11 +429,13 @@
     for line in (1, 2, 3):
         send_line(1, line)
     own_table.wait()
+    forward(1, 0)
     finish_lines(0)
     quarter = SLOTS // 4
     for line in range(4):
         lax.fori_loop(line * quarter, (line + 1) * quarter, multiply(0), 0, unroll=4)
-        forward(1, line)
+        if line < 3:
+            forward(1, line + 1)
     for core_index in range(2):
         for n in range(channels // group):
             sum_lags(0, core_index, n, keep)
@@ -492,6 +494,11 @@
 def identity(n):
     diagonal = lax.broadcasted_iota(jnp.int32, (n, n), 0) == lax.broadcasted_iota(jnp.int32, (n, n), 1)
     return jnp.where(diagonal, 1.0, 0.0).astype(jnp.bfloat16)
+
+
+def turn_kernel(landed, out):
+    for s in range(out.shape[0]):
+        out[s] = landed[s].astype(jnp.float32).T.astype(out.dtype)
 
 
 def body(strain, source_block, source_offset, window_valid):
@@ -536,8 +543,15 @@
         cost_estimate=pl.CostEstimate(flops=4 * 256 * 4096 * 2048, bytes_accessed=20 * 2**20, transcendentals=0),
     )(tiles, jnp.asarray(row_tables()), jnp.asarray(short_dft(), dtype=bf16),
       jnp.asarray(lag_table(), dtype=bf16), source_block, source_offset, window_valid)
-    rows = landed.reshape(-1, 2 * SIDE * channels, LAGS)
-    return jnp.einsum("tu,scu->stc", jnp.eye(LAGS, dtype=bf16), rows, preferred_element_type=f32).astype(bf16)
+    sources, steps = SRC_BLOCK // (2 * SIDE), 2
+    rows = 2 * SIDE * channels
+    return pl.pallas_call(
+        turn_kernel,
+        grid=(steps,),
+        in_specs=[pl.BlockSpec((sources // steps, rows, LAGS), lambda i: (i, 0, 0))],
+        out_specs=pl.BlockSpec((sources // steps, LAGS, rows), lambda i: (i, 0, 0)),
+        out_shape=jax.ShapeDtypeStruct((sources, LAGS, rows), bf16),
+    )(landed.reshape(sources, rows, LAGS))
 
 
 def solution(mesh):

time: 102 us -> 103 us (level)
  Pallas kernels: 97.8 us -> 101 us
  matrix products: 1.69 us -> 0 us
  local copies, waits for them, and re-layouts: 1.31 us -> 0 us
    pallas_call x0 -> x1, Pallas kernels: none -> 2.27 us  [body(): pl.pallas_call(turn_kernel, grid=(steps,), in_specs=[pl.BlockSpec((source...]
    dot_general x1 -> x0, matrix products: 1.69 us -> none  [body(): jnp.einsum('tu,scu->stc', jnp.eye(LAGS, dtype=bf16), rows, preferred_elem...]
    convert_element_type x1 -> x0, local copies, waits for them, and re-layouts: 1.31 us -> none  [body(): jnp.einsum('tu,scu->stc', jnp.eye(LAGS, dtype=bf16), rows, preferred_elem...]
    pallas_call x1, Pallas kernels: 97.8 us -> 98.9 us  [body(): pl.pallas_call(kernel, in_specs=[anywhere] * 4 + [scalars] * 3, out_specs...]
where the time goes in v12:
time: 103 us; the launch traced here: 102 us
  Pallas kernels  101 us (98%)
  between operations  1.31 us (1%)
    pallas_call x1, Pallas kernels, body(): pl.pallas_call(kernel, in_specs=[anywhere] * 4 + [scalars] * 3, out_specs...  98.9 us
    pallas_call x1, Pallas kernels, body(): pl.pallas_call(turn_kernel, grid=(steps,), in_specs=[pl.BlockSpec((source...  2.27 us

profile of v12, /device:TPU:1, one launch (start us, length us, event | category | flops | bytes accessed | tf_op | source)
XLA Modules:
  0.0 102.5 jit_solution(15256099772733920189)
XLA Ops:
  1.3 98.9 %shard_map.73 = bf16[16,8,16,256]{3,2,1,0:T(8,128)(2,1)} custom-call(f32[4352,128]{1,0:T(8,128)} %bitcast.7, f32[96,128]{1,0:T(8,128)} %constant.6.clone.rows_hbm, bf16[128,256]{1,0:T(8,128)(2,1)} %constant.7.clone.dft_hbm, bf16[2,256,2048]{2,1,0:T(8,128)(2,1)} %constant.8.clone.tables, s32[1]{0:T(128)S(6)} %copy.8.block, s32[1]{0:T(128)S(6)} %copy.9.offset, ...), custom_call_target="tpu_custom_call" | custom-call | flops 8589934592 | bytes 20971520 | tf_op jit(solution)/shard_map/pallas_call | solution.py:514
  100.2 2.3 %shard_map.74 = bf16[16,256,128]{2,1,0:T(8,128)(2,1)} custom-call(bf16[16,128,256]{2,1,0:T(8,128)(2,1)} %bitcast.6), custom_call_target="tpu_custom_call" | custom-call | tf_op jit(solution)/shard_map/pallas_call | solution.py:548

commit v13 on v12

--- a/solution.py
+++ b/solution.py
@@ -429,13 +429,11 @@
     for line in (1, 2, 3):
         send_line(1, line)
     own_table.wait()
-    forward(1, 0)
     finish_lines(0)
     quarter = SLOTS // 4
     for line in range(4):
         lax.fori_loop(line * quarter, (line + 1) * quarter, multiply(0), 0, unroll=4)
-        if line < 3:
-            forward(1, line + 1)
+        forward(1, line)
     for core_index in range(2):
         for n in range(channels // group):
             sum_lags(0, core_index, n, keep)

time: 103 us -> 101 us (0.981)
    pallas_call x1, Pallas kernels: 98.9 us -> 97.8 us  [body(): pl.pallas_call(kernel, in_specs=[anywhere] * 4 + [scalars] * 3, out_specs...]
where the time goes in v13:
time: 101 us
  Pallas kernels  100 us (99%)
  between operations  1.31 us (1%)
    pallas_call x1, Pallas kernels, body(): pl.pallas_call(kernel, in_specs=[anywhere] * 4 + [scalars] * 3, out_specs...  97.8 us
    pallas_call x1, Pallas kernels, body(): pl.pallas_call(turn_kernel, grid=(steps,), in_specs=[pl.BlockSpec((source...  2.27 us

profile of v13, /device:TPU:1, one launch (start us, length us, event | category | flops | bytes accessed | tf_op | source)
XLA Modules:
  0.0 101.3 jit_solution(12918434784272832065)
XLA Ops:
  1.3 97.8 %shard_map.73 = bf16[16,8,16,256]{3,2,1,0:T(8,128)(2,1)} custom-call(f32[4352,128]{1,0:T(8,128)} %bitcast.7, f32[96,128]{1,0:T(8,128)} %constant.6.clone.rows_hbm, bf16[128,256]{1,0:T(8,128)(2,1)} %constant.7.clone.dft_hbm, bf16[2,256,2048]{2,1,0:T(8,128)(2,1)} %constant.8.clone.tables, s32[1]{0:T(128)S(6)} %copy.8.block, s32[1]{0:T(128)S(6)} %copy.9.offset, ...), custom_call_target="tpu_custom_call" | custom-call | flops 8589934592 | bytes 20971520 | tf_op jit(solution)/shard_map/pallas_call | solution.py:512
  99.1 2.3 %shard_map.74 = bf16[16,256,128]{2,1,0:T(8,128)(2,1)} custom-call(bf16[16,128,256]{2,1,0:T(8,128)(2,1)} %bitcast.6), custom_call_target="tpu_custom_call" | custom-call | tf_op jit(solution)/shard_map/pallas_call | solution.py:546
